TPU v7x, 512 devices: a whole 4x4x16 slice. The times are simulated.
512 devices in a mesh: row: 16 (over x, y_hi, core), col: 32 (over y_lo, z).
Axes of the slice: x: 4, y: 4 (y_hi: 2, y_lo: 2; y = y_hi * 2 + y_lo), z: 16, core: 2. Of those that a mesh axis runs over, the one named last changes fastest.
Arguments:
- hidden_in: bfloat16 [2048, 4096], P('row', 'col'), may hold values from -16 to 16
- norm_gain: bfloat16 [4096], P('col'), may hold values from 0.3 to 3
- w_query: bfloat16 [4096, 4096], P('row', 'col'), may hold values from -0.09375 to 0.09375
- w_key: bfloat16 [4096, 4096], P('row', 'col'), may hold values from -0.09375 to 0.09375
- w_value: bfloat16 [4096, 4096], P('row', 'col'), may hold values from -0.09375 to 0.09375
- w_out: bfloat16 [4096, 4096], P('row', 'col'), may hold values from -0.09375 to 0.09375
- packet_ids: int32 [2048], replicated, may hold values from 0 to 63, never falling along the last dimension, each value on 1 to 96 neighbouring positions
- grad_out: bfloat16 [2048, 4096], P('row', 'col'), may hold values from -6 to 6
Outputs:
- mixed: bfloat16 [2048, 4096], P('row', 'col')
- grad_x: float32 [2048, 4096], P('row', 'col')
- grad_gain: float32 [4096], P('col')
- grad_w_query: float32 [4096, 4096], P('row', 'col')
- grad_w_key: float32 [4096, 4096], P('row', 'col')
- grad_w_value: float32 [4096, 4096], P('row', 'col')
- grad_w_out: float32 [4096, 4096], P('row', 'col')
Inputs may be any that keep to these rules, and one draw needn't show every extreme that they name: `packet_ids`: packet ids never fall along the tokens; each of the 64 packets holds 1 to 96 tokens, at least one exactly 96.
All inputs are finite; a program needn't handle non-finite values.
Results may differ from a plain program's by a relative error of at most 0.035.
Values may be sent and summed in bfloat16 or wider, within the bound.
No kernel may reach another device: no remote copies, remote signals or barrier semaphores. Data moves between devices by JAX's collectives and lax.ppermute only.
A program may use at most 64 MiB of HBM per device.

v0:
```python
import jax
import jax.numpy as jnp
from jax import lax
from jax.sharding import PartitionSpec as P

D = 4096
HD = 128


norm_eps = 1e-05


def local(hidden_in, norm_gain, w_query, w_key, w_value, w_out, packet_ids, grad_out):
    tok_rows, feat_cols = hidden_in.shape
    tok_total = packet_ids.shape[0]
    head_count = feat_cols // HD
    score_scale = HD ** (-0.5)
    x_full, gain_full = (
        lax.all_gather(hidden_in, "col", axis=1, tiled=True),
        lax.all_gather(norm_gain, "col", axis=0, tiled=True),
    )
    query_full, key_full, value_full, out_full = (
        lax.all_gather(w_query, "row", axis=0, tiled=True),
        lax.all_gather(w_key, "row", axis=0, tiled=True),
        lax.all_gather(w_value, "row", axis=0, tiled=True),
        lax.all_gather(w_out, "row", axis=0, tiled=True),
    )
    x_wide = x_full.astype(jnp.float32)
    recip = lax.rsqrt(jnp.mean(x_wide * x_wide, axis=1) + norm_eps)
    normed = (x_wide * recip[:, None] * gain_full.astype(jnp.float32)).astype(jnp.bfloat16)
    query = jnp.dot(normed, query_full, preferred_element_type=jnp.float32).astype(jnp.bfloat16)
    key = jnp.dot(normed, key_full, preferred_element_type=jnp.float32).astype(jnp.bfloat16)
    value = jnp.dot(normed, value_full, preferred_element_type=jnp.float32).astype(jnp.bfloat16)
    keys_all, values_all = (
        lax.all_gather(key, "row", axis=0, tiled=True),
        lax.all_gather(value, "row", axis=0, tiled=True),
    )
    first_row = lax.axis_index("row") * tok_rows
    packet_own = lax.dynamic_slice_in_dim(packet_ids, first_row, tok_rows)
    allowed = packet_ids[None, :] <= packet_own[:, None]
    query_three = query.reshape(tok_rows, head_count, HD)
    keys_three = keys_all.reshape(tok_total, head_count, HD)
    values_three = values_all.reshape(tok_total, head_count, HD)
    scores = (
        jnp.einsum("qhd,khd->hqk", query_three, keys_three, preferred_element_type=jnp.float32)
        * score_scale
    )
    scores = jnp.where(allowed[None], scores, -1e30)
    row_max = jnp.max(scores, axis=2)
    exponent = jnp.where(allowed[None], jnp.exp(scores - row_max[:, :, None]), 0.0)
    row_total = jnp.sum(exponent, axis=2)
    probs = exponent / row_total[:, :, None]
    probs_low = probs.astype(jnp.bfloat16)
    attended = (
        jnp.einsum("hqk,khd->qhd", probs_low, values_three, preferred_element_type=jnp.float32)
        .astype(jnp.bfloat16)
        .reshape(tok_rows, feat_cols)
    )
    heads_wide = lax.all_gather(attended, "col", axis=1, tiled=True)
    own_float = hidden_in.astype(jnp.float32)
    mixed = (own_float + jnp.dot(heads_wide, out_full, preferred_element_type=jnp.float32)).astype(
        jnp.bfloat16
    )
    grads_tall = lax.all_gather(grad_out, "row", axis=0, tiled=True)
    heads_tall, normed_tall = (
        lax.all_to_all(heads_wide, "row", split_axis=1, concat_axis=0, tiled=True),
        lax.all_to_all(normed, "row", split_axis=1, concat_axis=0, tiled=True),
    )
    grad_w_out = jnp.einsum("ta,tn->an", heads_tall, grads_tall, preferred_element_type=jnp.float32)
    head_part = jnp.einsum("tn,an->ta", grad_out, out_full, preferred_element_type=jnp.float32)
    grad_heads = lax.psum_scatter(
        head_part.astype(jnp.bfloat16), "col", scatter_dimension=1, tiled=True
    )
    grad_three = grad_heads.reshape(tok_rows, head_count, HD)
    dprob = jnp.einsum("qhd,khd->hqk", grad_three, values_three, preferred_element_type=jnp.float32)
    row_delta = jnp.sum(dprob * probs, axis=2)
    dscore = (probs * (dprob - row_delta[:, :, None])).astype(jnp.bfloat16)
    grad_query = (
        (
            jnp.einsum("hqk,khd->qhd", dscore, keys_three, preferred_element_type=jnp.float32)
            * score_scale
        )
        .astype(jnp.bfloat16)
        .reshape(tok_rows, feat_cols)
    )
    key_part = (
        jnp.einsum("hqk,qhd->khd", dscore, query_three, preferred_element_type=jnp.float32)
        * score_scale
    )
    value_part = jnp.einsum(
        "hqk,qhd->khd", probs_low, grad_three, preferred_element_type=jnp.float32
    )
    key_sum, value_sum = (
        lax.psum_scatter(
            key_part.reshape(tok_total, feat_cols).astype(jnp.bfloat16),
            "row",
            scatter_dimension=0,
            tiled=True,
        ).astype(jnp.float32),
        lax.psum_scatter(
            value_part.reshape(tok_total, feat_cols).astype(jnp.bfloat16),
            "row",
            scatter_dimension=0,
            tiled=True,
        ).astype(jnp.float32),
    )
    grad_key = key_sum.astype(jnp.bfloat16)
    grad_value = value_sum.astype(jnp.bfloat16)
    input_part = jnp.einsum("to,ko->tk", grad_query, query_full, preferred_element_type=jnp.float32)
    input_part = input_part + jnp.einsum(
        "to,ko->tk", grad_key, key_full, preferred_element_type=jnp.float32
    )
    input_part = input_part + jnp.einsum(
        "to,ko->tk", grad_value, value_full, preferred_element_type=jnp.float32
    )
    grad_normed = lax.psum_scatter(
        input_part.astype(jnp.bfloat16), "col", scatter_dimension=1, tiled=True
    ).astype(jnp.float32)
    gq_tall, gk_tall, gv_tall = (
        lax.all_gather(grad_query, "row", axis=0, tiled=True),
        lax.all_gather(grad_key, "row", axis=0, tiled=True),
        lax.all_gather(grad_value, "row", axis=0, tiled=True),
    )
    grad_w_query = jnp.einsum("tk,to->ko", normed_tall, gq_tall, preferred_element_type=jnp.float32)
    grad_w_key = jnp.einsum("tk,to->ko", normed_tall, gk_tall, preferred_element_type=jnp.float32)
    grad_w_value = jnp.einsum("tk,to->ko", normed_tall, gv_tall, preferred_element_type=jnp.float32)
    scaled = grad_normed * norm_gain.astype(jnp.float32)
    feat_dot = lax.psum(jnp.sum(scaled * own_float, axis=1), "col")
    grad_gain = lax.psum(jnp.sum(grad_normed * own_float * recip[:, None], axis=0), "row")
    grad_x = (
        grad_out.astype(jnp.float32)
        + recip[:, None] * scaled
        - own_float * (recip * recip * recip * feat_dot / D)[:, None]
    )
    return (mixed, grad_x, grad_gain, grad_w_query, grad_w_key, grad_w_value, grad_w_out)


def solution(mesh):
    in_specs = (
        P("row", "col"),
        P("col"),
        P("row", "col"),
        P("row", "col"),
        P("row", "col"),
        P("row", "col"),
        P(),
        P("row", "col"),
    )
    out_specs = (
        P("row", "col"),
        P("row", "col"),
        P("col"),
        P("row", "col"),
        P("row", "col"),
        P("row", "col"),
        P("row", "col"),
    )
    return jax.shard_map(local, mesh=mesh, in_specs=in_specs, out_specs=out_specs, check_vma=False)
```

profile of v0, /device:TPU:1, one launch (start us, length us, event | category | flops | bytes accessed | tf_op | source)
XLA Modules:
  0.0 1078.8 jit_solution(12119141481336818201)
XLA Ops:
  7.9 1.5 copy.19
  9.5 0.7 all-gather.16.cloned.1.call-update
  11.4 55.7 %all-gather.2 = bf16[32,1,128]{2,1,0:T(2,128)(2,1)S(1)} all-gather(bf16[1,1,128]{2,1,0:T(2,128)(2,1)} %bitcast.88), channel_id=1, replica_groups=mesh['row'=16,'col'=32] {'col'}, dimensions={0}, use_global_device_ids=true | all-gather | bytes 8448 | tf_op jit(solution)/shard_map/all_gather | solution.py:20
  67.2 0.8 dynamic_slice.3
  67.9 9.5 all-gather.18.cloned.1.call-done
  77.4 1.7 convolution_convert_fusion
  79.1 1.3 copy.22
  80.5 108.2 %all-gather.10.cloned.1.call-done = bf16[128,4096]{0,1:T(8,128)(2,1)} async-done(((bf16[128,128]{0,1:T(8,128)(2,1)}), bf16[128,4096]{0,1:T(8,128)(2,1)}) %all-gather.10.cloned.1.call-update) | async-done | bytes 1048592 | tf_op jit(solution)/shard_map/all_gather | solution.py:19
  188.7 1.8 fusion.5
  190.5 2.5 fusion.7
  193.0 74.4 %all-gather.16.cloned.1.call-done = bf16[4096,128]{1,0:T(8,128)(2,1)} async-done(((bf16[256,128]{1,0:T(8,128)(2,1)}), bf16[4096,128]{1,0:T(8,128)(2,1)}) %all-gather.16.cloned.1.call-update) | async-done | bytes 1048592 | tf_op jit(solution)/shard_map/all_gather | solution.py:24
  267.4 2.0 convolution_convert_fusion.3
  269.5 22.9 %all_gather.45 = bf16[2048,128]{1,0:T(8,128)(2,1)S(1)} all-gather(bf16[128,128]{1,0:T(8,128)(2,1)S(1)} %convolution_convert_fusion.3), channel_id=1, replica_groups=mesh['row'=16,'col'=32] {'row'}, dimensions={0}, use_global_device_ids=true | all-gather | bytes 557056 | tf_op jit(solution)/shard_map/all_gather | solution.py:35
  292.4 37.5 %all-gather.14.cloned.1.call-done = bf16[4096,128]{1,0:T(8,128)(2,1)} async-done(((bf16[256,128]{1,0:T(8,128)(2,1)}), bf16[4096,128]{1,0:T(8,128)(2,1)}) %all-gather.14.cloned.1.call-update) | async-done | bytes 1048592 | tf_op jit(solution)/shard_map/all_gather | solution.py:23
  329.9 2.0 convolution_convert_fusion.4
  332.6 59.6 %all-gather.12.cloned.1.call-done = bf16[4096,128]{1,0:T(8,128)(2,1)} async-done(((bf16[256,128]{1,0:T(8,128)(2,1)}), bf16[4096,128]{1,0:T(8,128)(2,1)}) %all-gather.12.cloned.1.call-update) | async-done | bytes 1048592 | tf_op jit(solution)/shard_map/all_gather | solution.py:25
  392.3 2.0 convolution_convert_fusion.5
  394.3 22.9 %all_gather.42 = bf16[2048,128]{1,0:T(8,128)(2,1)S(1)} all-gather(bf16[128,128]{1,0:T(8,128)(2,1)S(1)} %convolution_convert_fusion.5), channel_id=1, replica_groups=mesh['row'=16,'col'=32] {'row'}, dimensions={0}, use_global_device_ids=true | all-gather | bytes 557056 | tf_op jit(solution)/shard_map/all_gather | solution.py:36
  417.2 88.4 %reduce-scatter.13.cloned.1.call-done = bf16[128,128]{1,0:T(8,128)(2,1)} async-done(((bf16[4096,128]{1,0:T(8,128)(2,1)}), bf16[128,128]{1,0:T(8,128)(2,1)}) %reduce-scatter.13.cloned.1.call-update) | async-done | bytes 32784
  505.6 1.3 multiply_reduce_fusion
  507.4 1.0 copy.24
  508.8 1.0 copy.26
  509.9 1.0 fusion.10
  510.9 30.9 %all-to-all-start = ((bf16[128,16,256]{0,2,1:T(8,128)(2,1)}), bf16[128,16,256]{0,2,1:T(8,128)(2,1)}, u32[]{:S(2)}, u32[]{:S(2)}) async-start(bf16[128,16,256]{0,2,1:T(8,128)(2,1)} %bitcast.14), calls=%async_computation | async-start | bytes 2097152 | tf_op jit(solution)/shard_map/all_to_all | solution.py:67
  542.2 3.0 fusion.24
  545.2 67.1 %reduce-scatter.15.cloned.1.call-done = bf16[128,128]{1,0:T(8,128)(2,1)} async-done(((bf16[2048,128]{1,0:T(8,128)(2,1)}), bf16[128,128]{1,0:T(8,128)(2,1)}) %reduce-scatter.15.cloned.1.call-update) | async-done | bytes 32784
  612.3 2.0 convolution_add_fusion.1
  614.3 90.3 %reduce-scatter.17.cloned.1.call-done = bf16[128,128]{1,0:T(8,128)(2,1)} async-done(((bf16[2048,128]{1,0:T(8,128)(2,1)}), bf16[128,128]{1,0:T(8,128)(2,1)}) %reduce-scatter.17.cloned.1.call-update) | async-done | bytes 32784
  704.6 1.7 fusion
  706.3 1.3 copy.28
  707.7 26.9 %all_gather.51 = bf16[2048,128]{1,0:T(8,128)(2,1)} all-gather(bf16[128,128]{1,0:T(8,128)(2,1)S(1)} %copy-done.7), channel_id=1, replica_groups=mesh['row'=16,'col'=32] {'row'}, dimensions={0}, use_global_device_ids=true | all-gather | bytes 557056 | tf_op jit(solution)/shard_map/all_gather | solution.py:64
  734.6 1.5 copy.20
  736.1 21.4 %all-gather.1 = bf16[2048,1,128]{0,2,1:T(8,128)(2,1)S(1)} all-gather(bf16[128,1,128]{0,2,1:T(8,128)(2,1)S(1)} %bitcast.85), channel_id=3, replica_groups=mesh['row'=16,'col'=32] {'row'}, dimensions={0}, use_global_device_ids=true | all-gather | bytes 557056 | tf_op jit(solution)/shard_map/all_gather | solution.py:120
  757.6 1.1 fusion.14
  759.0 23.2 %all_gather.50 = bf16[2048,128]{0,1:T(8,128)(2,1)S(1)} all-gather(bf16[128,128]{0,1:T(8,128)(2,1)S(1)} %copy.27), channel_id=1, replica_groups=mesh['row'=16,'col'=32] {'row'}, dimensions={0}, use_global_device_ids=true | all-gather | bytes 557056 | tf_op jit(solution)/shard_map/all_gather | solution.py:122
  782.2 22.6 %all_gather.49 = bf16[2048,128]{0,1:T(8,128)(2,1)} all-gather(bf16[128,128]{0,1:T(8,128)(2,1)S(1)} %copy.25), channel_id=1, replica_groups=mesh['row'=16,'col'=32] {'row'}, dimensions={0}, use_global_device_ids=true | all-gather | bytes 557056 | tf_op jit(solution)/shard_map/all_gather | solution.py:121
  804.7 1.1 fusion.34
  805.8 15.0 %all-gather.20.cloned.1.call-done = bf16[128,1,4096]{0,2,1:T(8,128)(2,1)} async-done(((bf16[128,1,128]{0,2,1:T(8,128)(2,1)}), bf16[128,1,4096]{0,2,1:T(8,128)(2,1)}) %all-gather.20.cloned.1.call-update) | async-done | bytes 1048592 | tf_op jit(solution)/shard_map/all_gather | solution.py:59
  820.8 2.3 copy.21
  823.1 27.1 %all-to-all-start.1 = ((bf16[128,16,256]{2,0,1:T(8,128)(2,1)}), bf16[128,16,256]{2,0,1:T(8,128)(2,1)}, u32[]{:S(2)}, u32[]{:S(2)}) async-start(bf16[128,16,256]{2,0,1:T(8,128)(2,1)} %copy.21), calls=%async_computation.1 | async-start | bytes 2097152 | tf_op jit(solution)/shard_map/all_to_all | solution.py:66
  850.3 2.2 fusion.33
  852.4 1.1 fusion.8
  853.5 96.7 %reduce-scatter.19.cloned.1.call-done = bf16[128,128]{1,0:T(8,128)(2,1)} async-done(((bf16[4096,128]{1,0:T(8,128)(2,1)}), bf16[128,128]{1,0:T(8,128)(2,1)}) %reduce-scatter.19.cloned.1.call-update) | async-done | bytes 32784
  950.3 0.9 copy.29
  951.3 47.3 %psum.14 = f32[128]{0:T(128)S(1)} all-reduce(f32[128]{0:T(128)S(1)} %get-tuple-element.8), channel_id=1, replica_groups=mesh['row'=16,'col'=32] {'col'}, use_global_device_ids=true, to_apply=%region_9.10 | all-reduce | flops 128 | bytes 1024 | tf_op jit(solution)/shard_map/psum | solution.py:128
  998.6 70.3 %psum.15 = f32[128]{0:T(128)} all-reduce(f32[128]{0:T(128)S(1)} %get-tuple-element.7), channel_id=1, replica_groups=mesh['row'=16,'col'=32] {'row'}, use_global_device_ids=true, to_apply=%region_11.12 | all-reduce | flops 128 | bytes 1024 | tf_op jit(solution)/shard_map/psum | solution.py:129
  1068.9 0.7 fusion.20
  1069.7 2.4 fusion.35
  (60 shorter events, 4.6 us)
Async XLA Ops:
  7.2 70.2 %all-gather.18.cloned.1.call-start = ((), (), s32[]{:S(2)}) async-start(), calls=%async_computation.10 | async-start | bytes 1114112 | tf_op jit(solution)/shard_map/all_gather | solution.py:26
  7.9 180.8 %all-gather.10.cloned.1.call-start = ((), (), s32[]{:S(2)}) async-start(), calls=%async_computation.6 | async-start | bytes 1081344 | tf_op jit(solution)/shard_map/all_gather | solution.py:19
  9.4 258.0 %all-gather.16.cloned.1.call-start = ((), (), s32[]{:S(2)}) async-start(), calls=%async_computation.9 | async-start | bytes 1114112 | tf_op jit(solution)/shard_map/all_gather | solution.py:24
  10.2 319.7 %all-gather.14.cloned.1.call-start = ((), (), s32[]{:S(2)}) async-start(), calls=%async_computation.8 | async-start | bytes 1114112 | tf_op jit(solution)/shard_map/all_gather | solution.py:23
  10.8 381.5 %all-gather.12.cloned.1.call-start = ((), (), s32[]{:S(2)}) async-start(), calls=%async_computation.7 | async-start | bytes 1114112 | tf_op jit(solution)/shard_map/all_gather | solution.py:25
  11.3 494.2 %reduce-scatter.13.cloned.1.call-start = ((), (), s32[]{:S(2)}) async-start(), calls=%async_computation.12 | async-start | bytes 1081344
  80.4 531.9 %reduce-scatter.15.cloned.1.call-start = ((), (), s32[]{:S(2)}) async-start(), calls=%async_computation.13 | async-start | bytes 557056
  193.0 138.9 %copy-start.10 = (s32[2048]{0:T(1024)S(1)}, s32[2048]{0:T(1024)}, u32[]{:S(2)}) copy-start(s32[2048]{0:T(1024)} %param.14) | copy-start | bytes 24580
  417.2 89.7 %copy-start.3 = (bf16[2048,128]{1,0:T(8,128)(2,1)}, bf16[2048,128]{1,0:T(8,128)(2,1)S(1)}, u32[]{:S(2)}) copy-start(bf16[2048,128]{1,0:T(8,128)(2,1)S(1)} %all_gather.42) | copy-start | bytes 1572868
  506.9 1.6 copy-start.11
  508.4 1.5 copy-start.4
  508.4 196.2 %reduce-scatter.17.cloned.1.call-start = ((), (), s32[]{:S(2)}) async-start(), calls=%async_computation.14 | async-start | bytes 557056
  509.8 311.0 %all-gather.20.cloned.1.call-start = ((), (), s32[]{:S(2)}) async-start(), calls=%async_computation.11 | async-start | bytes 1081344 | tf_op jit(solution)/shard_map/all_gather | solution.py:59
  510.9 223.7 %all-to-all-start = ((bf16[128,16,256]{0,2,1:T(8,128)(2,1)}), bf16[128,16,256]{0,2,1:T(8,128)(2,1)}, u32[]{:S(2)}, u32[]{:S(2)}) async-start(bf16[128,16,256]{0,2,1:T(8,128)(2,1)} %bitcast.14), calls=%async_computation | async-start | bytes 2097152 | tf_op jit(solution)/shard_map/all_to_all | solution.py:67
  541.8 70.5 %copy-start = (bf16[4096,128]{1,0:T(8,128)(2,1)S(1)}, bf16[4096,128]{1,0:T(8,128)(2,1)}, u32[]{:S(2)}) copy-start(bf16[4096,128]{1,0:T(8,128)(2,1)} %all-gather.16.cloned.1.call-done) | copy-start | bytes 3145732
  541.8 408.5 %reduce-scatter.19.cloned.1.call-start = ((), (), s32[]{:S(2)}) async-start(), calls=%async_computation.15 | async-start | bytes 1081344
  706.3 1.4 copy-start.12
  706.3 1.4 copy-start.7
  734.6 24.1 %copy-start.9 = (bf16[128,128]{1,0:T(8,128)(2,1)S(1)}, bf16[128,128]{1,0:T(8,128)(2,1)}, u32[]{:S(2)}) copy-start(bf16[128,128]{1,0:T(8,128)(2,1)} %reduce-scatter.17.cloned.1.call-done) | copy-start | bytes 98308
  734.6 24.2 %copy-start.8 = (bf16[128,128]{1,0:T(8,128)(2,1)S(1)}, bf16[128,128]{1,0:T(8,128)(2,1)}, u32[]{:S(2)}) copy-start(bf16[128,128]{1,0:T(8,128)(2,1)} %reduce-scatter.15.cloned.1.call-done) | copy-start | bytes 98308
  823.1 29.3 %copy-start.1 = (bf16[4096,128]{1,0:T(8,128)(2,1)S(1)}, bf16[4096,128]{1,0:T(8,128)(2,1)}, u32[]{:S(2)}) copy-start(bf16[4096,128]{1,0:T(8,128)(2,1)} %all-gather.18.cloned.1.call-done) | copy-start | bytes 3145732
  823.1 29.3 %copy-start.2 = (bf16[128,1,4096]{0,2,1:T(8,128)(2,1)S(1)}, bf16[128,1,4096]{0,2,1:T(8,128)(2,1)}, u32[]{:S(2)}) copy-start(bf16[128,1,4096]{0,2,1:T(8,128)(2,1)} %all-gather.20.cloned.1.call-done) | copy-start | bytes 3145732
  823.1 29.3 %copy-start.6 = (bf16[128,128]{1,0:T(8,128)(2,1)S(1)}, bf16[128,128]{1,0:T(8,128)(2,1)}, u32[]{:S(2)}) copy-start(bf16[128,128]{1,0:T(8,128)(2,1)} %param.8) | copy-start | bytes 98308
  823.1 246.5 %all-to-all-start.1 = ((bf16[128,16,256]{2,0,1:T(8,128)(2,1)}), bf16[128,16,256]{2,0,1:T(8,128)(2,1)}, u32[]{:S(2)}, u32[]{:S(2)}) async-start(bf16[128,16,256]{2,0,1:T(8,128)(2,1)} %copy.21), calls=%async_computation.1 | async-start | bytes 2097152 | tf_op jit(solution)/shard_map/all_to_all | solution.py:66
  852.4 217.2 %copy-start.5 = (bf16[2048,128]{1,0:T(8,128)(2,1)S(1)}, bf16[2048,128]{1,0:T(8,128)(2,1)}, u32[]{:S(2)}) copy-start(bf16[2048,128]{1,0:T(8,128)(2,1)} %all_gather.51) | copy-start | bytes 1572868
Sparse Core Ops, SparseCore 0:
  11.3 66.0 all-gather.17
  80.1 108.6 all-gather.9
  192.0 75.4 all-gather.15
  270.6 59.2 all-gather.13
  333.0 59.2 all-gather.11
  394.9 110.6 reduce-scatter.12
  510.9 101.3 reduce-scatter.14
  616.9 87.6 reduce-scatter.16
  707.5 113.3 all-gather.19
  823.7 126.5 reduce-scatter.18
where the time goes:
time: 1080 us
  waiting for transfers between devices  649 us (60%)
  blocking collectives  313 us (29%)
  starting transfers between devices  58.4 us (5%)
  matrix products  25.9 us (2%)
  between operations  14.4 us (1%)
  local copies, waits for them, and re-layouts  11.8 us (1%)
    unnamed x14, waiting for transfers between devices  345 us
    all_gather x1, waiting for transfers between devices, local(): lax.all_gather(hidden_in, 'col', axis=1, tiled=True)  108 us
    all_gather x1, waiting for transfers between devices, local(): lax.all_gather(w_key, 'row', axis=0, tiled=True)  74.4 us
    psum x1, blocking collectives, local(): lax.psum(jnp.sum(grad_normed * own_float * recip[:, None], axis=0), 'row')  70.3 us
    all_gather x1, waiting for transfers between devices, local(): lax.all_gather(w_value, 'row', axis=0, tiled=True)  59.6 us
    all_gather x1, blocking collectives, local(): lax.all_gather(norm_gain, 'col', axis=0, tiled=True)  55.7 us
    psum x1, blocking collectives, local(): feat_dot = lax.psum(jnp.sum(scaled * own_float, axis=1), 'col')  47.3 us
    all_gather x1, waiting for transfers between devices, local(): lax.all_gather(w_query, 'row', axis=0, tiled=True)  37.5 us
  transfers between devices with their start and end apart: 12, of which 10 were waited for; matrix products, arithmetic and copies ran while one was open for 4% of the time, Pallas kernels for 0%

commit v1 on v0

v1 whole, which is shorter than its diff:
```python
import jax
import jax.numpy as jnp
from jax import lax
from jax.experimental import pallas as pl
from jax.experimental.pallas import tpu as pltpu
from jax.sharding import PartitionSpec as P

D = 4096
HD = 128
TOK = 2048
BLOCK = 256
OVER = 128
SCALE = HD ** (-0.5)
MASKED = -1e30
norm_eps = 1e-05

F32 = jnp.float32
BF16 = jnp.bfloat16


def col_at(a, h, l):
    return a * 16 + 2 * h + l


FAR = [[col_at(a, h, l) for h in range(8)] for a in range(2) for l in range(2)]
NEAR = [[col_at(a, h, l) for a in range(2) for l in range(2)] for h in range(8)]
CHIPS = [[2 * k + core for k in range(8)] for core in range(2)]
CORE_SWAP = [(r, r ^ 1) for r in range(16)]
TURN = [(r * 32 + c, (c // 2) * 32 + 2 * r + c % 2) for r in range(16) for c in range(32)]
TURN_ODD = [(r * 32 + c, (c // 2) * 32 + 2 * r + 1 - c % 2) for r in range(16) for c in range(32)]


def mm(a, b):
    return jnp.dot(a, b, preferred_element_type=F32)


def mm_nt(a, b):
    return lax.dot_general(a, b, (((1,), (1,)), ((), ())), preferred_element_type=F32)


def mm_tn(a, b):
    return lax.dot_general(a, b, (((0,), (0,)), ((), ())), preferred_element_type=F32)


def spread(x, axis, groups):
    n = len(groups[0])
    wide = jnp.broadcast_to(x[None], (n,) + x.shape)
    return lax.all_to_all(wide, axis, 0, 0, tiled=True, axis_index_groups=groups)


def flip(x):
    return x.astype(F32).T.astype(BF16)


def project_kernel(core_ref, wide, own, other, heads, both, recip_out):
    core = core_ref[0]
    squares = jnp.zeros((128, 128), F32)
    for a in range(2):
        for l in range(2):
            for h in range(8):
                x = wide[a, l, h, 0:128, :].astype(F32)
                squares = squares + x * x
    recip = lax.rsqrt(jnp.sum(squares, axis=1, keepdims=True) / D + norm_eps)
    recip_out[...] = recip
    qkv = jnp.zeros((128, 3 * HD), F32)
    grad = jnp.zeros((128, HD), F32)
    for k in range(8):
        for src, flag in ((own, core), (other, 1 - core)):
            h = 2 * (k % 4) + flag
            normed, go = [], []
            for l in range(2):
                x = wide[k // 4, l, h, 0:128, :].astype(F32)
                gain = wide[k // 4, l, h, 256:272, :].astype(F32)[0:1, :]
                normed.append((x * recip * gain).astype(BF16))
                go.append(wide[k // 4, l, h, 128:256, :])
            normed = jnp.concatenate(normed, axis=1)
            go = jnp.concatenate(go, axis=1)
            both[2 * k + flag, :, 0:256] = normed
            both[2 * k + flag, :, 256:512] = go
            qkv = qkv + mm(normed, src[k, :, 0 : 3 * HD])
            grad = grad + mm(go, src[k, :, 3 * HD :])
    heads[:, 0 : 3 * HD] = qkv.astype(BF16)
    heads[:, 3 * HD :] = grad.astype(BF16)


def project(core, wide, own, other):
    vmem = pl.BlockSpec(memory_space=pltpu.VMEM)
    return pl.pallas_call(
        project_kernel,
        out_shape=(
            jax.ShapeDtypeStruct((128, 4 * HD), BF16),
            jax.ShapeDtypeStruct((16, 128, 512), BF16),
            jax.ShapeDtypeStruct((128, 1), F32),
        ),
        in_specs=[pl.BlockSpec(memory_space=pltpu.SMEM), vmem, vmem, vmem],
        out_specs=(vmem, vmem, vmem),
        compiler_params=pltpu.CompilerParams(vmem_limit_bytes=48 * 1024 * 1024),
        name="project",
    )(core[None], wide, own, other)


def dot_rows(dot):
    high = dot.astype(BF16)
    low = (dot - high.astype(F32)).astype(BF16)
    at = lax.broadcasted_iota(jnp.int32, (16, 128), 0)
    wide = jnp.where(at == 0, high.astype(F32), jnp.where(at == 1, low.astype(F32), 0.0))
    return wide.astype(BF16)


def parts_kernel(place, grads, att, wide, w_own, w_other, parts):
    core, row = place[0], place[1]
    here = pl.ds(pl.multiple_of(row * 128, 128), 128)
    grad, attended = grads[here, :], att[here, :]
    dots = jnp.zeros((128, 128), F32)
    for k in range(8):
        for src, flag in ((w_own, core), (w_other, 1 - core)):
            h = 2 * (k % 4) + flag
            back = mm_nt(grad, src[k, :, 0 : 3 * HD]).astype(BF16)
            mixed = mm_nt(attended, src[k, :, 3 * HD :]).astype(BF16)
            for l in range(2):
                cut = slice(l * 128, (l + 1) * 128)
                x = wide[k // 4, l, h, 0:128, :].astype(F32)
                gain = wide[k // 4, l, h, 256:272, :].astype(F32)[0:1, :]
                dots = dots + back[:, cut].astype(F32) * gain * x
                parts[2 * (k // 4) + l, h, 0:128, :] = back[:, cut]
                parts[2 * (k // 4) + l, h, 128:256, :] = mixed[:, cut]
    extra = dot_rows(jnp.sum(dots.T, axis=0, keepdims=True))
    for n in range(4):
        for h in range(8):
            parts[n, h, 256:272, :] = extra


def to_parts(core, row, grads, att, wide, w_own, w_other):
    vmem = pl.BlockSpec(memory_space=pltpu.VMEM)
    return pl.pallas_call(
        parts_kernel,
        out_shape=jax.ShapeDtypeStruct((4, 8, 272, 128), BF16),
        in_specs=[pl.BlockSpec(memory_space=pltpu.SMEM)] + [vmem] * 5,
        out_specs=vmem,
        compiler_params=pltpu.CompilerParams(vmem_limit_bytes=48 * 1024 * 1024),
        name="to_parts",
    )(jnp.stack([core, row]), grads, att, wide, w_own, w_other)


def merge_kernel(parts, out):
    for h in range(8):
        total = parts[0, h].astype(F32)
        for n in range(1, 4):
            total = total + parts[n, h].astype(F32)
        out[h, 0:256, :] = total[0:256].astype(BF16)
        out[h, 256:272, :] = dot_rows(total[256:257] + total[257:258])


def merge(parts):
    vmem = pl.BlockSpec(memory_space=pltpu.VMEM)
    return pl.pallas_call(
        merge_kernel,
        out_shape=jax.ShapeDtypeStruct((8, 272, 128), BF16),
        in_specs=[vmem],
        out_specs=vmem,
        compiler_params=pltpu.CompilerParams(vmem_limit_bytes=48 * 1024 * 1024),
        name="merge",
    )(parts)


def finish_kernel(parts, hidden, gain_in, recip_in, grad_out, mixed, grad_x, gain_part):
    total = parts[0].astype(F32)
    for n in range(1, 8):
        total = total + parts[n].astype(F32)
    grad_normed = total[0:128]
    dot = total[256:257] + total[257:258]
    dot = jnp.broadcast_to(dot, (128, 128)).T
    x = hidden[...].astype(F32)
    recip = recip_in[...]
    mixed[...] = (x + total[128:256]).astype(BF16)
    scaled = grad_normed * gain_in[...].astype(F32)
    grad_x[...] = grad_out[...].astype(F32) + recip * scaled - x * (recip * recip * recip * dot / D)
    part = jnp.sum(grad_normed * x * recip, axis=0, keepdims=True)
    for n in range(16):
        gain_part[n] = part


def finish(parts, hidden, gain, recip, grad_out):
    vmem = pl.BlockSpec(memory_space=pltpu.VMEM)
    return pl.pallas_call(
        finish_kernel,
        out_shape=(
            jax.ShapeDtypeStruct((128, 128), BF16),
            jax.ShapeDtypeStruct((128, 128), F32),
            jax.ShapeDtypeStruct((16, 1, 128), F32),
        ),
        in_specs=[vmem] * 5,
        out_specs=(vmem, vmem, vmem),
        name="finish",
    )(parts, hidden, gain[None, :], recip, grad_out)


def attention_kernel(
    core_ref, ids_row, ids_col, own, other, grads, att,
    q_s, k_s, v_s, g_s, q_t, k_t, v_t, g_t, s_s, e_s, dk_s, dv_s,
):
    core = core_ref[0]
    for k in range(8):
        for src, flag in ((own, core), (other, 1 - core)):
            at = pl.ds(pl.multiple_of((2 * k + flag) * 128, 128), 128)
            for n, (flat, turned) in enumerate(((q_s, q_t), (k_s, k_t), (v_s, v_t), (g_s, g_t))):
                piece = src[k, :, n * 128 : (n + 1) * 128]
                flat[at, :] = piece
                turned[:, at] = flip(piece)
    dk_s[...] = jnp.zeros_like(dk_s)
    dv_s[...] = jnp.zeros_like(dv_s)
    for i in range(TOK // BLOCK):
        base = i * BLOCK
        here = slice(base, base + BLOCK)
        tiles = [(j * BLOCK, BLOCK) for j in range(i + 1)]
        if base + BLOCK < TOK:
            tiles.append((base + BLOCK, OVER))
        query_t = q_t[:, here]
        top = jnp.full((1, BLOCK), MASKED, F32)
        for start, size in tiles:
            score = mm(k_s[start : start + size, :], query_t)
            if start >= base:
                seen = ids_col[start : start + size, :] <= ids_row[:, here]
                score = jnp.where(seen, score, MASKED)
            s_s[start : start + size, :] = score
            top = jnp.maximum(top, jnp.max(score, axis=0, keepdims=True))
        total = jnp.zeros((1, BLOCK), F32)
        att_t = jnp.zeros((HD, BLOCK), F32)
        for start, size in tiles:
            part = jnp.exp((s_s[start : start + size, :] - top) * SCALE)
            s_s[start : start + size, :] = part
            total = total + jnp.sum(part, axis=0, keepdims=True)
            low = part.astype(BF16)
            e_s[start : start + size, :] = low
            att_t = att_t + mm(v_t[:, start : start + size], low)
        inverse = 1.0 / total
        att_t = att_t * inverse
        att[here, :] = att_t.T.astype(BF16)
        grad_t = (g_t[:, here].astype(F32) * inverse).astype(BF16)
        grad_t_wide = grad_t.astype(F32)
        grad = grad_t_wide.T.astype(BF16)
        delta = jnp.sum(grad_t_wide * att_t, axis=0, keepdims=True)
        query = q_s[here, :]
        dq_t = jnp.zeros((HD, BLOCK), F32)
        for start, size in tiles:
            at = slice(start, start + size)
            dprob = mm(v_s[at, :], grad_t)
            dscore = (s_s[at, :] * (dprob - delta)).astype(BF16)
            dq_t = dq_t + mm(k_t[:, at], dscore)
            dk_s[at, :] += mm(dscore, query)
            dv_s[at, :] += mm(e_s[at, :], grad)
        grads[here, 0:HD] = (dq_t * SCALE).T.astype(BF16)
    grads[:, HD : 2 * HD] = (dk_s[...] * SCALE).astype(BF16)
    grads[:, 2 * HD : 3 * HD] = dv_s[...].astype(BF16)


def attention(core, packet_ids, own, other):
    low = pltpu.VMEM((TOK, HD), BF16)
    low_t = pltpu.VMEM((HD, TOK), BF16)
    vmem = pl.BlockSpec(memory_space=pltpu.VMEM)
    return pl.pallas_call(
        attention_kernel,
        out_shape=(
            jax.ShapeDtypeStruct((TOK, 3 * HD), BF16),
            jax.ShapeDtypeStruct((TOK, HD), BF16),
        ),
        in_specs=[pl.BlockSpec(memory_space=pltpu.SMEM), vmem, vmem, vmem, vmem],
        out_specs=(vmem, vmem),
        scratch_shapes=[low] * 4
        + [low_t] * 4
        + [
            pltpu.VMEM((TOK, BLOCK), F32),
            pltpu.VMEM((TOK, BLOCK), BF16),
            pltpu.VMEM((TOK, HD), F32),
            pltpu.VMEM((TOK, HD), F32),
        ],
        compiler_params=pltpu.CompilerParams(vmem_limit_bytes=48 * 1024 * 1024),
        name="attention",
    )(core[None], packet_ids[None, :], packet_ids[:, None], own, other)


def halves(core, own, other):
    return jnp.where(core == 0, own, other), jnp.where(core == 0, other, own)


def local(hidden_in, norm_gain, w_query, w_key, w_value, w_out, packet_ids, grad_out):
    row = lax.axis_index("row")
    col = lax.axis_index("col")
    core = row % 2
    odd = col % 2

    half = lax.dynamic_slice_in_dim(w_out, odd * 128, 128, 0)
    half_odd = lax.dynamic_slice_in_dim(w_out, (1 - odd) * 128, 128, 0)
    got = lax.ppermute(half, ("row", "col"), TURN)
    got_odd = lax.ppermute(half_odd, ("row", "col"), TURN_ODD)
    out_n = jnp.concatenate(halves(odd, got, got_odd), axis=1).T
    weights = jnp.concatenate([w_query, w_key, w_value, out_n], axis=1)
    w_own = spread(weights, "row", CHIPS)
    w_other = lax.ppermute(w_own, "row", CORE_SWAP)

    gain_rows = jnp.broadcast_to(norm_gain[None], (16, 128))
    pair = jnp.concatenate([hidden_in, grad_out, gain_rows], axis=0)
    far = lax.all_gather(pair, "col", axis=0, axis_index_groups=FAR)
    wide = spread(far.reshape(8, 272, 128), "col", NEAR).reshape(2, 2, 8, 272, 128)
    heads, both, recip = project(core, wide, w_own, w_other)
    heads_own = spread(heads, "row", CHIPS)

    both, heads_own = lax.optimization_barrier((both, heads_own))
    both = lax.all_to_all(both, "row", 0, 0, tiled=True)

    heads_other = lax.ppermute(heads_own, "row", CORE_SWAP)
    grads, attended = attention(core, packet_ids, heads_own, heads_other)

    parts = to_parts(core, row, grads, attended, wide, w_own, w_other)
    parts, both = lax.optimization_barrier((parts, both))
    tall = both.reshape(TOK, 512)
    grad_o = mm_tn(attended, tall[:, 256:])
    here, there = halves(odd, grad_o[:, :128], grad_o[:, 128:])
    parts, here, there = lax.optimization_barrier((parts, here, there))
    parts = lax.all_to_all(parts, "col", 0, 0, tiled=True, axis_index_groups=NEAR)
    parts = lax.all_to_all(merge(parts), "col", 0, 0, tiled=True, axis_index_groups=FAR)
    mixed, grad_x, gain_part = finish(parts, hidden_in, norm_gain, recip, grad_out)
    gain_all = lax.all_to_all(gain_part, "row", 0, 0, tiled=True)
    grad_gain = jnp.sum(gain_all, axis=(0, 1))

    grad_w = mm_tn(tall[:, :256], grads)
    got = lax.ppermute(here, ("row", "col"), TURN)
    got_odd = lax.ppermute(there, ("row", "col"), TURN_ODD)
    grad_w_out = jnp.concatenate(halves(odd, got, got_odd), axis=0)
    return (
        mixed,
        grad_x,
        grad_gain,
        grad_w[:, :128],
        grad_w[:, 128:256],
        grad_w[:, 256:],
        grad_w_out,
    )


def solution(mesh):
    tiled = P("row", "col")
    in_specs = (tiled, P("col"), tiled, tiled, tiled, tiled, P(), tiled)
    out_specs = (tiled, tiled, P("col"), tiled, tiled, tiled, tiled)
    return jax.shard_map(local, mesh=mesh, in_specs=in_specs, out_specs=out_specs, check_vma=False)
```

time: 1080 us -> 268 us (0.25)
  waiting for transfers between devices: 649 us -> 42.3 us
  blocking collectives: 313 us -> 72.6 us
  starting transfers between devices: 58.4 us -> 102 us
  Pallas kernels: 0 us -> 29.1 us
  matrix products: 25.9 us -> 3.7 us
  between operations: 14.4 us -> 0.92 us
    unnamed x14 -> x0, waiting for transfers between devices: 345 us -> none
    all_gather x6 -> x0, waiting for transfers between devices: 304 us -> none  [the longest x1 108 us: local(): lax.all_gather(hidden_in, 'col', axis=1, tiled=True)]
    all_gather x7 -> x1, blocking collectives: 196 us -> 27.5 us  [local(): far = lax.all_gather(pair, 'col', axis=0, axis_index_groups=FAR)]
    psum x2 -> x0, blocking collectives: 118 us -> none  [the longest x1 70.3 us: local(): lax.psum(jnp.sum(grad_normed * own_float * recip[:, None], axis=0), 'row')]
    all_to_all x0 -> x2, blocking collectives: none -> 45.1 us  [the longest x1 29.9 us: local(): lax.all_to_all(parts, 'col', 0, 0, tiled=True, axis_index_groups=NEAR)]
    ppermute x0 -> x6, starting transfers between devices: none -> 29.2 us  [the longest x1 8.81 us: local(): w_other = lax.ppermute(w_own, 'row', CORE_SWAP)]
    pallas_call x0 -> x5, Pallas kernels: none -> 29.1 us  [the longest x1 17.4 us: attention(): pl.pallas_call(attention_kernel, out_shape=(jax.ShapeDtypeStruct((TOK, 3...]
    dot_general x18 -> x2, matrix products: 25.9 us -> 3.7 us  [mm_tn(): lax.dot_general(a, b, (((0,), (0,)), ((), ())), preferred_element_type=F32)]
  transfers between devices with their start and end apart: 12 -> 11, of which waited for: 10 -> 7; matrix products, arithmetic and copies ran while one was open for 4% -> 3% of each run, Pallas kernels for 0% -> 8%
where the time goes in v1:
time: 268 us; the launch traced here: 266 us
  starting transfers between devices  102 us (38%)
  blocking collectives  72.6 us (27%)
  waiting for transfers between devices  42.3 us (16%)
  Pallas kernels  29.1 us (11%)
  local copies, waits for them, and re-layouts  13.8 us (5%)
  matrix products  3.7 us (1%)
    all_to_all x1, blocking collectives, local(): lax.all_to_all(parts, 'col', 0, 0, tiled=True, axis_index_groups=NEAR)  29.9 us
    all_gather x1, blocking collectives, local(): far = lax.all_gather(pair, 'col', axis=0, axis_index_groups=FAR)  27.5 us
    all_to_all x1, starting transfers between devices, local(): gain_all = lax.all_to_all(gain_part, 'row', 0, 0, tiled=True)  26.6 us
    all_to_all x2, starting transfers between devices, spread(): lax.all_to_all(wide, axis, 0, 0, tiled=True, axis_index_groups=groups)  26.5 us
    pallas_call x1, Pallas kernels, attention(): pl.pallas_call(attention_kernel, out_shape=(jax.ShapeDtypeStruct((TOK, 3...  17.4 us
    all_to_all x1, blocking collectives, spread(): lax.all_to_all(wide, axis, 0, 0, tiled=True, axis_index_groups=groups)  15.3 us
    all_to_all x2, waiting for transfers between devices, spread(): lax.all_to_all(wide, axis, 0, 0, tiled=True, axis_index_groups=groups)  14.6 us
    ppermute x1, waiting for transfers between devices, local(): got = lax.ppermute(here, ('row', 'col'), TURN)  14.4 us
  transfers between devices with their start and end apart: 11, of which 7 were waited for; matrix products, arithmetic and copies ran while one was open for 3% of the time, Pallas kernels for 8%

profile of v1, /device:TPU:1, one launch (start us, length us, event | category | flops | bytes accessed | tf_op | source)
XLA Modules:
  0.0 265.9 jit_solution(1315755295721251887)
XLA Ops:
  0.7 0.8 constant_dynamic-slice_fusion.1
  1.4 6.3 %collective-permute-start = (bf16[128,128]{1,0:T(8,128)(2,1)S(1)}, bf16[128,128]{1,0:T(8,128)(2,1)S(1)}, u32[]{:S(2)}, u32[]{:S(2)}) collective-permute-start(bf16[128,128]{1,0:T(8,128)(2,1)S(1)} %get-tuple-element.46), channel_id=1, source_target_pairs={{0,0},{1,1},{2,32},{3,33},{4,64},{5,65},{6,96},{7,97},{8,128},{9,1... | collective-permute-start | bytes 98312 | tf_op jit(solution)/shard_map/ppermute | solution.py:294
  7.7 3.3 %collective-permute-start.1 = (bf16[128,128]{1,0:T(8,128)(2,1)S(1)}, bf16[128,128]{1,0:T(8,128)(2,1)S(1)}, u32[]{:S(2)}, u32[]{:S(2)}) collective-permute-start(bf16[128,128]{1,0:T(8,128)(2,1)S(1)} %get-tuple-element.47), channel_id=1, source_target_pairs={{0,1},{1,0},{2,33},{3,32},{4,65},{5,64},{6,97},{7,96},{8,129},{9,1... | collective-permute-start | bytes 98312 | tf_op jit(solution)/shard_map/ppermute | solution.py:295
  11.0 0.9 copy.19
  12.0 0.9 copy.20
  12.9 0.9 copy.21
  13.9 1.4 collective-permute-done.1
  15.4 0.1 copy.22
  15.5 1.5 broadcast_in_dim.18
  17.0 21.2 %all-to-all-start.1 = ((bf16[8,256,512]{2,1,0:T(8,128)(2,1)}), bf16[8,256,512]{2,1,0:T(8,128)(2,1)S(1)}, u32[]{:S(2)}, u32[]{:S(2)}) async-start(bf16[8,256,512]{2,1,0:T(8,128)(2,1)} %broadcast_in_dim.18), calls=%async_computation.1 | async-start | bytes 4194304 | tf_op jit(solution)/shard_map/all_to_all | solution.py:48
  38.3 27.5 %all-gather = bf16[2176,128]{1,0:T(8,128)(2,1)S(1)} all-gather(bf16[272,128]{1,0:T(8,128)(2,1)S(1)} %pad_maximum_fusion.2), channel_id=2, replica_groups={{0,2,4,6,8,10,12,14},{1,3,5,7,9,11,13,15},{16,18,20,22,24,26,28,30},{17..., dimensions={0}, use_global_device_ids=true | all-gather | bytes 626688 | tf_op jit(solution)/shard_map/all_gather | solution.py:303
  65.7 0.0 all-to-all-done.1.own.w_own
  65.8 1.7 broadcast_in_dim.17
  67.4 5.3 %all-to-all-start = ((bf16[4,8,272,128]{3,2,1,0:T(8,128)(2,1)}), bf16[4,8,272,128]{3,2,1,0:T(8,128)(2,1)}, u32[]{:S(2)}, u32[]{:S(2)}) async-start(bf16[4,8,272,128]{3,2,1,0:T(8,128)(2,1)} %broadcast_in_dim.17), calls=%async_computation | async-start | bytes 4456448 | tf_op jit(solution)/shard_map/all_to_all | solution.py:48
  72.7 8.8 %collective-permute-start.2 = (bf16[8,256,512]{2,1,0:T(8,128)(2,1)S(1)}, bf16[8,256,512]{2,1,0:T(8,128)(2,1)}, u32[]{:S(2)}, u32[]{:S(2)}) collective-permute-start(bf16[8,256,512]{2,1,0:T(8,128)(2,1)S(1)} %all-to-all-done.1.own.w_own), channel_id=1, source_target_pairs={{0,32},{32,0},{64,96},{96,64},{128,160},{160,128},{192,224},{224,1... | collective-permute-start | bytes 6291464 | tf_op jit(solution)/shard_map/ppermute | solution.py:299
  81.6 3.9 %collective-permute-done.2.other.w_other = bf16[8,256,512]{2,1,0:T(8,128)(2,1)} collective-permute-done((bf16[8,256,512]{2,1,0:T(8,128)(2,1)S(1)}, bf16[8,256,512]{2,1,0:T(8,128)(2,1)}, u32[]{:S(2)}, u32[]{:S(2)}) %collective-permute-start.2) | collective-permute-done | bytes 2097184 | tf_op jit(solution)/shard_map/ppermute | solution.py:299
  85.4 14.6 %all-to-all-done = bf16[4,8,272,128]{3,2,1,0:T(8,128)(2,1)} async-done(((bf16[4,8,272,128]{3,2,1,0:T(8,128)(2,1)}), bf16[4,8,272,128]{3,2,1,0:T(8,128)(2,1)}, u32[]{:S(2)}, u32[]{:S(2)}) %all-to-all-start) | async-done | bytes 2228256 | tf_op jit(solution)/shard_map/all_to_all | solution.py:48
  100.0 3.6 %project.1 = (bf16[128,512]{1,0:T(8,128)(2,1)S(1)}, bf16[16,128,512]{2,1,0:T(8,128)(2,1)S(1)}, f32[128,1]{1,0:T(8,128)S(1)}) custom-call(s32[1]{0:T(128)} %bitcast.core_ref, bf16[2,2,8,272,128]{4,3,2,1,0:T(8,128)(2,1)} %bitcast.5.wide, bf16[8,256,512]{2,1,0:T(8,128)(2,1)S(1)} %all-to-all-done.1.own.w_own, ...), custom_call_target="tpu_custom_call" | custom-call | tf_op jit(solution)/shard_map/project/pallas_call | solution.py:88
  103.6 0.0 copy-start.5
  103.6 0.6 copy-done.5
  104.3 0.1 broadcast_in_dim.19
  104.3 15.3 %all_to_all.35.own = bf16[8,128,512]{2,1,0:T(8,128)(2,1)S(1)} all-to-all(bf16[8,128,512]{2,1,0:T(8,128)(2,1)S(1)} %broadcast_in_dim.19), channel_id=1, replica_groups={{0,64,128,192,256,320,384,448},{32,96,160,224,288,352,416,480},{1,65,12..., dimensions={0} | all-to-all | bytes 2097152 | tf_op jit(solution)/shard_map/all_to_all | solution.py:48
  119.6 9.4 %all-to-all-start.3 = ((bf16[16,128,512]{2,1,0:T(8,128)(2,1)}), bf16[16,128,512]{2,1,0:T(8,128)(2,1)}, u32[]{:S(2)}, u32[]{:S(2)}) async-start(bf16[16,128,512]{2,1,0:T(8,128)(2,1)} %copy-done.3), calls=%async_computation.3 | async-start | bytes 4194304 | tf_op jit(solution)/shard_map/all_to_all | solution.py:309
  129.0 2.4 collective-permute-start.3
  131.4 1.4 copy.23.ids_col
  132.8 0.1 pad_add_fusion.place
  132.9 0.8 collective-permute-done.3.other
  133.7 1.2 copy-done.2
  134.9 17.4 %attention.1 = (bf16[2048,384]{1,0:T(8,128)(2,1)S(1)}, bf16[2048,128]{1,0:T(8,128)(2,1)S(1)}) custom-call(s32[1]{0:T(128)} %bitcast.core_ref, s32[1,2048]{1,0:T(1,128)S(1)} %bitcast.13, s32[2048,1]{1,0:T(8,128)S(1)} %copy-done.2, bf16[8,128,512]{2,1,0:T(8,128)(2,1)S(1)} %all_to_all.35.own, bf16[8,128,512]{2,1,0:T(8,128)(2,1)} %collective-permute-done.3.other), custom_call_target="tpu_custom_call" | custom-call | tf_op jit(solution)/shard_map/attention/pallas_call | solution.py:261
  152.4 5.1 %to_parts.1 = bf16[4,8,272,128]{3,2,1,0:T(8,128)(2,1)} custom-call(s32[2]{0:T(128)S(1)} %pad_add_fusion.place, bf16[2048,384]{1,0:T(8,128)(2,1)S(1)} %get-tuple-element.25.grads, bf16[2048,128]{1,0:T(8,128)(2,1)S(1)} %get-tuple-element.26.att, bf16[2,2,8,272,128]{4,3,2,1,0:T(8,128)(2,1)} %bitcast.5.wide, bf16[8,256,512]{2,1,0:T(8,128)(2,1)S(1)} %all-to-all-done.1.own.w_own, ...), custom_call_target="tpu_custom_call" | custom-call | tf_op jit(solution)/shard_map/to_parts/pallas_call | solution.py:135
  157.5 1.2 copy-done
  158.7 0.8 copy-done.4
  159.5 1.7 fusion.2
  161.2 29.9 %all_to_all.36.parts = bf16[4,8,272,128]{3,2,1,0:T(8,128)(2,1)S(1)} all-to-all(bf16[4,8,272,128]{3,2,1,0:T(8,128)(2,1)} %to_parts.1), channel_id=1, replica_groups={{0,1,16,17},{2,3,18,19},{4,5,20,21},{6,7,22,23},{8,9,24,25},{10,11,26,2..., dimensions={0} | all-to-all | bytes 4456448 | tf_op jit(solution)/shard_map/all_to_all | solution.py:320
  191.1 1.1 merge.1
  192.1 10.5 %all-to-all-start.5 = ((bf16[8,272,128]{2,1,0:T(8,128)(2,1)}), bf16[8,272,128]{2,1,0:T(8,128)(2,1)S(1)}, u32[]{:S(2)}, u32[]{:S(2)}) async-start(bf16[8,272,128]{2,1,0:T(8,128)(2,1)} %merge.1), calls=%async_computation.5 | async-start | bytes 1114112 | tf_op jit(solution)/shard_map/all_to_all | solution.py:321
  202.6 6.2 %collective-permute-start.4 = (f32[128,128]{1,0:T(8,128)S(1)}, f32[128,128]{1,0:T(8,128)S(1)}, u32[]{:S(2)}, u32[]{:S(2)}) collective-permute-start(f32[128,128]{1,0:T(8,128)S(1)} %get-tuple-element.35), channel_id=1, source_target_pairs={{0,0},{1,1},{2,32},{3,33},{4,64},{5,65},{6,96},{7,97},{8,128},{9,1... | collective-permute-start | bytes 196616 | tf_op jit(solution)/shard_map/ppermute | solution.py:327
  208.8 2.3 collective-permute-start.5
  211.1 2.0 fusion
  213.1 0.8 fusion.4
  213.8 14.4 %collective-permute-done.4 = f32[128,128]{1,0:T(8,128)S(1)} collective-permute-done((f32[128,128]{1,0:T(8,128)S(1)}, f32[128,128]{1,0:T(8,128)S(1)}, u32[]{:S(2)}, u32[]{:S(2)}) %collective-permute-start.4) | collective-permute-done | bytes 65568 | tf_op jit(solution)/shard_map/ppermute | solution.py:327
  228.2 0.9 collective-permute-done.5
  229.1 0.8 copy-done.7
  229.9 1.9 finish.1
  231.8 26.6 %all-to-all-start.6 = ((f32[16,1,128]{2,1,0:T(1,128)}), f32[16,1,128]{2,1,0:T(1,128)S(1)}, u32[]{:S(2)}, u32[]{:S(2)}) async-start(f32[16,1,128]{2,1,0:T(1,128)} %get-tuple-element.34), calls=%async_computation.6 | async-start | bytes 16384 | tf_op jit(solution)/shard_map/all_to_all | solution.py:323
  258.3 0.7 pad_maximum_fusion.1
  259.0 6.3 %all-to-all-done.6 = f32[16,1,128]{2,1,0:T(1,128)S(1)} async-done(((f32[16,1,128]{2,1,0:T(1,128)}), f32[16,1,128]{2,1,0:T(1,128)S(1)}, u32[]{:S(2)}, u32[]{:S(2)}) %all-to-all-start.6) | async-done | bytes 8224 | tf_op jit(solution)/shard_map/all_to_all | solution.py:323
  265.3 0.5 reduce_sum.9
  (26 shorter events, 0.1 us)
Async XLA Ops:
  1.4 12.4 %collective-permute-start = (bf16[128,128]{1,0:T(8,128)(2,1)S(1)}, bf16[128,128]{1,0:T(8,128)(2,1)S(1)}, u32[]{:S(2)}, u32[]{:S(2)}) collective-permute-start(bf16[128,128]{1,0:T(8,128)(2,1)S(1)} %get-tuple-element.46), channel_id=1, source_target_pairs={{0,0},{1,1},{2,32},{3,33},{4,64},{5,65},{6,96},{7,97},{8,128},{9,1... | collective-permute-start | bytes 98312 | tf_op jit(solution)/shard_map/ppermute | solution.py:294
  7.7 7.6 %collective-permute-start.1 = (bf16[128,128]{1,0:T(8,128)(2,1)S(1)}, bf16[128,128]{1,0:T(8,128)(2,1)S(1)}, u32[]{:S(2)}, u32[]{:S(2)}) collective-permute-start(bf16[128,128]{1,0:T(8,128)(2,1)S(1)} %get-tuple-element.47), channel_id=1, source_target_pairs={{0,1},{1,0},{2,33},{3,32},{4,65},{5,64},{6,97},{7,96},{8,129},{9,1... | collective-permute-start | bytes 98312 | tf_op jit(solution)/shard_map/ppermute | solution.py:295
  17.0 21.2 %copy-start.10 = (bf16[128]{0:T(256)(128)(2,1)S(1)}, bf16[128]{0:T(256)(128)(2,1)}, u32[]{:S(2)}) copy-start(bf16[128]{0:T(256)(128)(2,1)} %param.9) | copy-start | bytes 772
  17.0 21.2 %copy-start.8 = (bf16[128,128]{1,0:T(8,128)(2,1)S(1)}, bf16[128,128]{1,0:T(8,128)(2,1)}, u32[]{:S(2)}) copy-start(bf16[128,128]{1,0:T(8,128)(2,1)} %grad_out.1) | copy-start | bytes 98308
  17.0 21.2 %copy-start.9 = (bf16[128,128]{1,0:T(8,128)(2,1)S(1)}, bf16[128,128]{1,0:T(8,128)(2,1)}, u32[]{:S(2)}) copy-start(bf16[128,128]{1,0:T(8,128)(2,1)} %hidden.1) | copy-start | bytes 98308
  17.0 48.7 %all-to-all-start.1 = ((bf16[8,256,512]{2,1,0:T(8,128)(2,1)}), bf16[8,256,512]{2,1,0:T(8,128)(2,1)S(1)}, u32[]{:S(2)}, u32[]{:S(2)}) async-start(bf16[8,256,512]{2,1,0:T(8,128)(2,1)} %broadcast_in_dim.18), calls=%async_computation.1 | async-start | bytes 4194304 | tf_op jit(solution)/shard_map/all_to_all | solution.py:48
  67.4 32.6 %all-to-all-start = ((bf16[4,8,272,128]{3,2,1,0:T(8,128)(2,1)}), bf16[4,8,272,128]{3,2,1,0:T(8,128)(2,1)}, u32[]{:S(2)}, u32[]{:S(2)}) async-start(bf16[4,8,272,128]{3,2,1,0:T(8,128)(2,1)} %broadcast_in_dim.17), calls=%async_computation | async-start | bytes 4456448 | tf_op jit(solution)/shard_map/all_to_all | solution.py:48
  72.7 12.7 %collective-permute-start.2 = (bf16[8,256,512]{2,1,0:T(8,128)(2,1)S(1)}, bf16[8,256,512]{2,1,0:T(8,128)(2,1)}, u32[]{:S(2)}, u32[]{:S(2)}) collective-permute-start(bf16[8,256,512]{2,1,0:T(8,128)(2,1)S(1)} %all-to-all-done.1.own.w_own), channel_id=1, source_target_pairs={{0,32},{32,0},{64,96},{96,64},{128,160},{160,128},{192,224},{224,1... | collective-permute-start | bytes 6291464 | tf_op jit(solution)/shard_map/ppermute | solution.py:299
  103.6 0.6 copy-start.5
  104.2 15.4 %copy-start.3 = (bf16[16,128,512]{2,1,0:T(8,128)(2,1)}, bf16[16,128,512]{2,1,0:T(8,128)(2,1)S(1)}, u32[]{:S(2)}) copy-start(bf16[16,128,512]{2,1,0:T(8,128)(2,1)S(1)} %get-tuple-element.27) | copy-start | bytes 6291460
  119.6 11.8 %copy-start.6 = (s32[2048]{0:T(1024)S(1)}, s32[2048]{0:T(1024)}, u32[]{:S(2)}) copy-start(s32[2048]{0:T(1024)} %param.14) | copy-start | bytes 24580
  119.6 39.8 %all-to-all-start.3 = ((bf16[16,128,512]{2,1,0:T(8,128)(2,1)}), bf16[16,128,512]{2,1,0:T(8,128)(2,1)}, u32[]{:S(2)}, u32[]{:S(2)}) async-start(bf16[16,128,512]{2,1,0:T(8,128)(2,1)} %copy-done.3), calls=%async_computation.3 | async-start | bytes 4194304 | tf_op jit(solution)/shard_map/all_to_all | solution.py:309
  129.0 4.7 %collective-permute-start.3 = (bf16[8,128,512]{2,1,0:T(8,128)(2,1)S(1)}, bf16[8,128,512]{2,1,0:T(8,128)(2,1)}, u32[]{:S(2)}, u32[]{:S(2)}) collective-permute-start(bf16[8,128,512]{2,1,0:T(8,128)(2,1)S(1)} %all_to_all.35.own), channel_id=1, source_target_pairs={{0,32},{32,0},{64,96},{96,64},{128,160},{160,128},{192,224},{224,1... | collective-permute-start | bytes 3145736 | tf_op jit(solution)/shard_map/ppermute | solution.py:311
  133.7 1.2 copy-start.2
  157.5 1.2 copy-start
  158.7 0.8 copy-start.4
  191.1 20.0 %copy-start.1 = (bf16[2048,384]{1,0:T(8,128)(2,1)S(1)}, bf16[2048,384]{1,0:T(8,128)(2,1)}, u32[]{:S(2)}) copy-start(bf16[2048,384]{1,0:T(8,128)(2,1)} %copy-done) | copy-start | bytes 4718596
  192.1 36.9 %all-to-all-start.5 = ((bf16[8,272,128]{2,1,0:T(8,128)(2,1)}), bf16[8,272,128]{2,1,0:T(8,128)(2,1)S(1)}, u32[]{:S(2)}, u32[]{:S(2)}) async-start(bf16[8,272,128]{2,1,0:T(8,128)(2,1)} %merge.1), calls=%async_computation.5 | async-start | bytes 1114112 | tf_op jit(solution)/shard_map/all_to_all | solution.py:321
  202.6 25.6 %collective-permute-start.4 = (f32[128,128]{1,0:T(8,128)S(1)}, f32[128,128]{1,0:T(8,128)S(1)}, u32[]{:S(2)}, u32[]{:S(2)}) collective-permute-start(f32[128,128]{1,0:T(8,128)S(1)} %get-tuple-element.35), channel_id=1, source_target_pairs={{0,0},{1,1},{2,32},{3,33},{4,64},{5,65},{6,96},{7,97},{8,128},{9,1... | collective-permute-start | bytes 196616 | tf_op jit(solution)/shard_map/ppermute | solution.py:327
  208.8 20.3 %collective-permute-start.5 = (f32[128,128]{1,0:T(8,128)S(1)}, f32[128,128]{1,0:T(8,128)S(1)}, u32[]{:S(2)}, u32[]{:S(2)}) collective-permute-start(f32[128,128]{1,0:T(8,128)S(1)} %get-tuple-element.36), channel_id=1, source_target_pairs={{0,1},{1,0},{2,33},{3,32},{4,65},{5,64},{6,97},{7,96},{8,129},{9,1... | collective-permute-start | bytes 196616 | tf_op jit(solution)/shard_map/ppermute | solution.py:328
  229.1 0.8 copy-start.7
  231.8 33.5 %all-to-all-start.6 = ((f32[16,1,128]{2,1,0:T(1,128)}), f32[16,1,128]{2,1,0:T(1,128)S(1)}, u32[]{:S(2)}, u32[]{:S(2)}) async-start(f32[16,1,128]{2,1,0:T(1,128)} %get-tuple-element.34), calls=%async_computation.6 | async-start | bytes 16384 | tf_op jit(solution)/shard_map/all_to_all | solution.py:323

commit v2 on v1

--- a/solution.py
+++ b/solution.py
@@ -27,7 +27,7 @@
 CHIPS = [[2 * k + core for k in range(8)] for core in range(2)]
 CORE_SWAP = [(r, r ^ 1) for r in range(16)]
 TURN = [(r * 32 + c, (c // 2) * 32 + 2 * r + c % 2) for r in range(16) for c in range(32)]
-TURN_ODD = [(r * 32 + c, (c // 2) * 32 + 2 * r + 1 - c % 2) for r in range(16) for c in range(32)]
+COL_SWAP = [(c, c ^ 1) for c in range(32)]
 
 
 def mm(a, b):
@@ -67,20 +67,23 @@
     for k in range(8):
         for src, flag in ((own, core), (other, 1 - core)):
             h = 2 * (k % 4) + flag
-            normed, go = [], []
+            normed = []
             for l in range(2):
                 x = wide[k // 4, l, h, 0:128, :].astype(F32)
                 gain = wide[k // 4, l, h, 256:272, :].astype(F32)[0:1, :]
                 normed.append((x * recip * gain).astype(BF16))
-                go.append(wide[k // 4, l, h, 128:256, :])
+                go = wide[k // 4, l, h, 128:256, :]
+                both[2 * k + flag, :, 256 + l * 128 : 384 + l * 128] = go
+                grad = grad + mm_nt(go, src[k, 768 + l * 128 : 896 + l * 128, :])
             normed = jnp.concatenate(normed, axis=1)
-            go = jnp.concatenate(go, axis=1)
             both[2 * k + flag, :, 0:256] = normed
-            both[2 * k + flag, :, 256:512] = go
-            qkv = qkv + mm(normed, src[k, :, 0 : 3 * HD])
-            grad = grad + mm(go, src[k, :, 3 * HD :])
+            qkv = qkv + mm(normed, projections(src, k))
     heads[:, 0 : 3 * HD] = qkv.astype(BF16)
     heads[:, 3 * HD :] = grad.astype(BF16)
+
+
+def projections(src, k):
+    return jnp.concatenate([src[k, n * 256 : (n + 1) * 256, :] for n in range(3)], axis=1)
 
 
 def project(core, wide, own, other):
@@ -105,41 +108,6 @@
     at = lax.broadcasted_iota(jnp.int32, (16, 128), 0)
     wide = jnp.where(at == 0, high.astype(F32), jnp.where(at == 1, low.astype(F32), 0.0))
     return wide.astype(BF16)
-
-
-def parts_kernel(place, grads, att, wide, w_own, w_other, parts):
-    core, row = place[0], place[1]
-    here = pl.ds(pl.multiple_of(row * 128, 128), 128)
-    grad, attended = grads[here, :], att[here, :]
-    dots = jnp.zeros((128, 128), F32)
-    for k in range(8):
-        for src, flag in ((w_own, core), (w_other, 1 - core)):
-            h = 2 * (k % 4) + flag
-            back = mm_nt(grad, src[k, :, 0 : 3 * HD]).astype(BF16)
-            mixed = mm_nt(attended, src[k, :, 3 * HD :]).astype(BF16)
-            for l in range(2):
-                cut = slice(l * 128, (l + 1) * 128)
-                x = wide[k // 4, l, h, 0:128, :].astype(F32)
-                gain = wide[k // 4, l, h, 256:272, :].astype(F32)[0:1, :]
-                dots = dots + back[:, cut].astype(F32) * gain * x
-                parts[2 * (k // 4) + l, h, 0:128, :] = back[:, cut]
-                parts[2 * (k // 4) + l, h, 128:256, :] = mixed[:, cut]
-    extra = dot_rows(jnp.sum(dots.T, axis=0, keepdims=True))
-    for n in range(4):
-        for h in range(8):
-            parts[n, h, 256:272, :] = extra
-
-
-def to_parts(core, row, grads, att, wide, w_own, w_other):
-    vmem = pl.BlockSpec(memory_space=pltpu.VMEM)
-    return pl.pallas_call(
-        parts_kernel,
-        out_shape=jax.ShapeDtypeStruct((4, 8, 272, 128), BF16),
-        in_specs=[pl.BlockSpec(memory_space=pltpu.SMEM)] + [vmem] * 5,
-        out_specs=vmem,
-        compiler_params=pltpu.CompilerParams(vmem_limit_bytes=48 * 1024 * 1024),
-        name="to_parts",
-    )(jnp.stack([core, row]), grads, att, wide, w_own, w_other)
 
 
 def merge_kernel(parts, out):
@@ -196,10 +164,19 @@
 
 
 def attention_kernel(
-    core_ref, ids_row, ids_col, own, other, grads, att,
+    place, ids, own, other, wide_in, w_own_in, w_other_in, grads, att, parts,
     q_s, k_s, v_s, g_s, q_t, k_t, v_t, g_t, s_s, e_s, dk_s, dv_s,
+    wide, w_own, w_other, sems,
 ):
-    core = core_ref[0]
+    core, row = place[0], place[1]
+    copies = [
+        pltpu.make_async_copy(src, dst, sems.at[n])
+        for n, (src, dst) in enumerate(
+            ((wide_in, wide), (w_own_in, w_own), (w_other_in, w_other))
+        )
+    ]
+    for copy in copies:
+        copy.start()
     for k in range(8):
         for src, flag in ((own, core), (other, 1 - core)):
             at = pl.ds(pl.multiple_of((2 * k + flag) * 128, 128), 128)
@@ -209,30 +186,43 @@
                 turned[:, at] = flip(piece)
     dk_s[...] = jnp.zeros_like(dk_s)
     dv_s[...] = jnp.zeros_like(dv_s)
-    for i in range(TOK // BLOCK):
+
+    def tiles_of(i):
+        tiles = [(j * BLOCK, BLOCK) for j in range(i + 1)]
+        if (i + 1) * BLOCK < TOK:
+            tiles.append(((i + 1) * BLOCK, OVER))
+        return tiles
+
+    def score_steps(i, state):
         base = i * BLOCK
         here = slice(base, base + BLOCK)
-        tiles = [(j * BLOCK, BLOCK) for j in range(i + 1)]
-        if base + BLOCK < TOK:
-            tiles.append((base + BLOCK, OVER))
-        query_t = q_t[:, here]
         top = jnp.full((1, BLOCK), MASKED, F32)
-        for start, size in tiles:
-            score = mm(k_s[start : start + size, :], query_t)
+        for start, size in tiles_of(i):
+            score = mm(k_s[start : start + size, :], q_t[:, here])
             if start >= base:
-                seen = ids_col[start : start + size, :] <= ids_row[:, here]
+                ids_tile = jnp.broadcast_to(ids[:, start : start + size], (8, size))
+                seen = ids_tile.T[:, 0:1] <= ids[:, here]
                 score = jnp.where(seen, score, MASKED)
-            s_s[start : start + size, :] = score
+            s_s[i % 2, start : start + size, :] = score
             top = jnp.maximum(top, jnp.max(score, axis=0, keepdims=True))
+            state["top"] = top
+            yield
+
+    def back_steps(i, state):
+        base = i * BLOCK
+        here = slice(base, base + BLOCK)
+        top = state["top"]
         total = jnp.zeros((1, BLOCK), F32)
         att_t = jnp.zeros((HD, BLOCK), F32)
-        for start, size in tiles:
-            part = jnp.exp((s_s[start : start + size, :] - top) * SCALE)
-            s_s[start : start + size, :] = part
+        for start, size in tiles_of(i):
+            at = slice(start, start + size)
+            part = jnp.exp((s_s[i % 2, at, :] - top) * SCALE)
+            s_s[i % 2, at, :] = part
             total = total + jnp.sum(part, axis=0, keepdims=True)
             low = part.astype(BF16)
-            e_s[start : start + size, :] = low
-            att_t = att_t + mm(v_t[:, start : start + size], low)
+            e_s[i % 2, at, :] = low
+            att_t = att_t + mm(v_t[:, at], low)
+            yield
         inverse = 1.0 / total
         att_t = att_t * inverse
         att[here, :] = att_t.T.astype(BF16)
@@ -242,41 +232,83 @@
         delta = jnp.sum(grad_t_wide * att_t, axis=0, keepdims=True)
         query = q_s[here, :]
         dq_t = jnp.zeros((HD, BLOCK), F32)
-        for start, size in tiles:
+        for start, size in tiles_of(i):
             at = slice(start, start + size)
             dprob = mm(v_s[at, :], grad_t)
-            dscore = (s_s[at, :] * (dprob - delta)).astype(BF16)
+            dscore = (s_s[i % 2, at, :] * (dprob - delta)).astype(BF16)
             dq_t = dq_t + mm(k_t[:, at], dscore)
             dk_s[at, :] += mm(dscore, query)
-            dv_s[at, :] += mm(e_s[at, :], grad)
+            dv_s[at, :] += mm(e_s[i % 2, at, :], grad)
+            yield
         grads[here, 0:HD] = (dq_t * SCALE).T.astype(BF16)
+
+    blocks = TOK // BLOCK
+    state = {}
+    for _ in score_steps(0, state):
+        pass
+    for i in range(blocks):
+        following = {}
+        ahead = score_steps(i + 1, following) if i + 1 < blocks else iter(())
+        for _ in back_steps(i, state):
+            next(ahead, None)
+        for _ in ahead:
+            pass
+        state = following
     grads[:, HD : 2 * HD] = (dk_s[...] * SCALE).astype(BF16)
     grads[:, 2 * HD : 3 * HD] = dv_s[...].astype(BF16)
 
-
-def attention(core, packet_ids, own, other):
+    for copy in copies:
+        copy.wait()
+    here = pl.ds(pl.multiple_of(row * 128, 128), 128)
+    grad, attended = grads[here, :], att[here, :]
+    dots = jnp.zeros((128, 128), F32)
+    for k in range(8):
+        for src, flag in ((w_own, core), (w_other, 1 - core)):
+            h = 2 * (k % 4) + flag
+            back = mm_nt(grad, projections(src, k)).astype(BF16)
+            for l in range(2):
+                cut = back[:, l * 128 : (l + 1) * 128]
+                x = wide[k // 4, l, h, 0:128, :].astype(F32)
+                gain = wide[k // 4, l, h, 256:272, :].astype(F32)[0:1, :]
+                dots = dots + cut.astype(F32) * gain * x
+                parts[2 * (k // 4) + l, h, 0:128, :] = cut
+                mixed = mm(attended, src[k, 768 + l * 128 : 896 + l * 128, :])
+                parts[2 * (k // 4) + l, h, 128:256, :] = mixed.astype(BF16)
+    extra = dot_rows(jnp.sum(dots.T, axis=0, keepdims=True))
+    for n in range(4):
+        for h in range(8):
+            parts[n, h, 256:272, :] = extra
+
+
+def attention(place, packet_ids, own, other, wide, w_own, w_other):
     low = pltpu.VMEM((TOK, HD), BF16)
     low_t = pltpu.VMEM((HD, TOK), BF16)
     vmem = pl.BlockSpec(memory_space=pltpu.VMEM)
+    anywhere = pl.BlockSpec(memory_space=pl.ANY)
     return pl.pallas_call(
         attention_kernel,
         out_shape=(
             jax.ShapeDtypeStruct((TOK, 3 * HD), BF16),
             jax.ShapeDtypeStruct((TOK, HD), BF16),
+            jax.ShapeDtypeStruct((4, 8, 272, 128), BF16),
         ),
-        in_specs=[pl.BlockSpec(memory_space=pltpu.SMEM), vmem, vmem, vmem, vmem],
-        out_specs=(vmem, vmem),
+        in_specs=[pl.BlockSpec(memory_space=pltpu.SMEM)] + [vmem] * 3 + [anywhere] * 3,
+        out_specs=(vmem, vmem, vmem),
         scratch_shapes=[low] * 4
         + [low_t] * 4
         + [
-            pltpu.VMEM((TOK, BLOCK), F32),
-            pltpu.VMEM((TOK, BLOCK), BF16),
+            pltpu.VMEM((2, TOK, BLOCK), F32),
+            pltpu.VMEM((2, TOK, BLOCK), BF16),
             pltpu.VMEM((TOK, HD), F32),
             pltpu.VMEM((TOK, HD), F32),
+            pltpu.VMEM(wide.shape, BF16),
+            pltpu.VMEM(w_own.shape, BF16),
+            pltpu.VMEM(w_other.shape, BF16),
+            pltpu.SemaphoreType.DMA((3,)),
         ],
-        compiler_params=pltpu.CompilerParams(vmem_limit_bytes=48 * 1024 * 1024),
+        compiler_params=pltpu.CompilerParams(vmem_limit_bytes=56 * 1024 * 1024),
         name="attention",
-    )(core[None], packet_ids[None, :], packet_ids[:, None], own, other)
+    )(place, packet_ids.astype(F32)[None, :], own, other, wide, w_own, w_other)
 
 
 def halves(core, own, other):
@@ -289,12 +321,12 @@
     core = row % 2
     odd = col % 2
 
-    half = lax.dynamic_slice_in_dim(w_out, odd * 128, 128, 0)
-    half_odd = lax.dynamic_slice_in_dim(w_out, (1 - odd) * 128, 128, 0)
-    got = lax.ppermute(half, ("row", "col"), TURN)
-    got_odd = lax.ppermute(half_odd, ("row", "col"), TURN_ODD)
-    out_n = jnp.concatenate(halves(odd, got, got_odd), axis=1).T
-    weights = jnp.concatenate([w_query, w_key, w_value, out_n], axis=1)
+    kept = lax.dynamic_slice_in_dim(w_out, odd * 128, 128, 0)
+    got = lax.dynamic_slice_in_dim(w_out, (1 - odd) * 128, 128, 0)
+    got = lax.ppermute(got, "col", COL_SWAP)
+    out_n = jnp.concatenate(halves(odd, kept, got), axis=0)
+    out_n = lax.ppermute(out_n, ("row", "col"), TURN)
+    weights = jnp.concatenate([w_query, w_key, w_value, out_n], axis=0)
     w_own = spread(weights, "row", CHIPS)
     w_other = lax.ppermute(w_own, "row", CORE_SWAP)
 
@@ -309,24 +341,26 @@
     both = lax.all_to_all(both, "row", 0, 0, tiled=True)
 
     heads_other = lax.ppermute(heads_own, "row", CORE_SWAP)
-    grads, attended = attention(core, packet_ids, heads_own, heads_other)
-
-    parts = to_parts(core, row, grads, attended, wide, w_own, w_other)
+    grads, attended, parts = attention(
+        jnp.stack([core, row]), packet_ids, heads_own, heads_other, wide, w_own, w_other
+    )
     parts, both = lax.optimization_barrier((parts, both))
-    tall = both.reshape(TOK, 512)
-    grad_o = mm_tn(attended, tall[:, 256:])
-    here, there = halves(odd, grad_o[:, :128], grad_o[:, 128:])
-    parts, here, there = lax.optimization_barrier((parts, here, there))
     parts = lax.all_to_all(parts, "col", 0, 0, tiled=True, axis_index_groups=NEAR)
     parts = lax.all_to_all(merge(parts), "col", 0, 0, tiled=True, axis_index_groups=FAR)
+    tall = both.reshape(TOK, 512)
+    grad_w = mm_tn(tall[:, :256], grads)
+    grad_o = mm_tn(tall[:, 256:], attended).astype(BF16)
+    parts, grad_w, grad_o = lax.optimization_barrier((parts, grad_w, grad_o))
+
     mixed, grad_x, gain_part = finish(parts, hidden_in, norm_gain, recip, grad_out)
     gain_all = lax.all_to_all(gain_part, "row", 0, 0, tiled=True)
     grad_gain = jnp.sum(gain_all, axis=(0, 1))
 
-    grad_w = mm_tn(tall[:, :256], grads)
-    got = lax.ppermute(here, ("row", "col"), TURN)
-    got_odd = lax.ppermute(there, ("row", "col"), TURN_ODD)
-    grad_w_out = jnp.concatenate(halves(odd, got, got_odd), axis=0)
+    grad_o = lax.ppermute(grad_o, ("row", "col"), TURN)
+    kept = lax.dynamic_slice_in_dim(grad_o, odd * 128, 128, 0)
+    got = lax.dynamic_slice_in_dim(grad_o, (1 - odd) * 128, 128, 0)
+    got = lax.ppermute(got, "col", COL_SWAP)
+    grad_w_out = jnp.concatenate(halves(odd, kept.T, got.T), axis=0).astype(F32)
     return (
         mixed,
         grad_x,

time: 268 us -> 252 us (0.940)
  starting transfers between devices: 102 us -> 84.5 us
  waiting for transfers between devices: 42.3 us -> 52 us
  local copies, waits for them, and re-layouts: 13.8 us -> 8.36 us
  Pallas kernels: 29.1 us -> 26.3 us
    all_to_all x1, waiting for transfers between devices: 0.01 us -> 22.2 us  [local(): lax.all_to_all(merge(parts), 'col', 0, 0, tiled=True, axis_index_groups=FAR)]
    all_to_all x1, starting transfers between devices: 26.6 us -> 5.47 us  [local(): gain_all = lax.all_to_all(gain_part, 'row', 0, 0, tiled=True)]
    ppermute x4, waiting for transfers between devices: 16.7 us -> 3.22 us  [the longest x1 1.93 us: local(): out_n = lax.ppermute(out_n, ('row', 'col'), TURN)]
    ppermute x4, starting transfers between devices: 18 us -> 26.2 us  [the longest x1 13.5 us: local(): grad_o = lax.ppermute(grad_o, ('row', 'col'), TURN)]
    pallas_call x1 -> x0, Pallas kernels: 5.11 us -> none  [to_parts(): pl.pallas_call(parts_kernel, out_shape=jax.ShapeDtypeStruct((4, 8, 272, 1...]
    unnamed x25, local copies, waits for them, and re-layouts: 7.47 us -> 3.29 us
    all_to_all x1, waiting for transfers between devices: 0.01 us -> 3.69 us  [local(): both = lax.all_to_all(both, 'row', 0, 0, tiled=True)]
    all_to_all x1, starting transfers between devices: 10.5 us -> 7.39 us  [local(): lax.all_to_all(merge(parts), 'col', 0, 0, tiled=True, axis_index_groups=FAR)]
  transfers between devices with their start and end apart: 11 -> 11, of which waited for: 7 -> 9; matrix products, arithmetic and copies ran while one was open for 3% -> 1% of each run, Pallas kernels for 8% -> 8%
where the time goes in v2:
time: 252 us; the launch traced here: 250 us
  starting transfers between devices  84.5 us (34%)
  blocking collectives  73.1 us (29%)
  waiting for transfers between devices  52 us (21%)
  Pallas kernels  26.3 us (10%)
  local copies, waits for them, and re-layouts  8.36 us (3%)
  other arithmetic  3.47 us (1%)
    all_to_all x1, blocking collectives, local(): lax.all_to_all(parts, 'col', 0, 0, tiled=True, axis_index_groups=NEAR)  29.2 us
    all_gather x1, blocking collectives, local(): far = lax.all_gather(pair, 'col', axis=0, axis_index_groups=FAR)  27.9 us
    all_to_all x2, starting transfers between devices, spread(): lax.all_to_all(wide, axis, 0, 0, tiled=True, axis_index_groups=groups)  24.8 us
    all_to_all x1, waiting for transfers between devices, local(): lax.all_to_all(merge(parts), 'col', 0, 0, tiled=True, axis_index_groups=FAR)  22.2 us
    pallas_call x1, Pallas kernels, attention(): pl.pallas_call(attention_kernel, out_shape=(jax.ShapeDtypeStruct((TOK, 3...  19.3 us
    all_to_all x1, blocking collectives, spread(): lax.all_to_all(wide, axis, 0, 0, tiled=True, axis_index_groups=groups)  16 us
    all_to_all x2, waiting for transfers between devices, spread(): lax.all_to_all(wide, axis, 0, 0, tiled=True, axis_index_groups=groups)  13.8 us
    ppermute x1, starting transfers between devices, local(): grad_o = lax.ppermute(grad_o, ('row', 'col'), TURN)  13.5 us
  transfers between devices with their start and end apart: 11, of which 9 were waited for; matrix products, arithmetic and copies ran while one was open for 1% of the time, Pallas kernels for 8%

profile of v2, /device:TPU:1, one launch (start us, length us, event | category | flops | bytes accessed | tf_op | source)
XLA Modules:
  0.0 249.9 jit_solution(3535328922446162362)
XLA Ops:
  0.6 0.8 constant_dynamic-slice_fusion.1
  1.4 4.4 %collective-permute-start = (bf16[128,128]{1,0:T(8,128)(2,1)S(1)}, bf16[128,128]{1,0:T(8,128)(2,1)S(1)}, u32[]{:S(2)}, u32[]{:S(2)}) collective-permute-start(bf16[128,128]{1,0:T(8,128)(2,1)S(1)} %constant_dynamic-slice_fusion.1), channel_id=1, source_target_pairs={{0,1},{1,0},{2,3},{3,2},{4,5},{5,4},{6,7},{7,6},{8,9},{9,8},{10,11... | collective-permute-start | bytes 98312 | tf_op jit(solution)/shard_map/ppermute | solution.py:326
  5.8 1.3 collective-permute-done
  7.1 0.8 broadcast_select_fusion.1
  7.9 6.4 %collective-permute-start.1 = (bf16[256,128]{1,0:T(8,128)(2,1)S(1)}, bf16[256,128]{1,0:T(8,128)(2,1)S(1)}, u32[]{:S(2)}, u32[]{:S(2)}) collective-permute-start(bf16[256,128]{1,0:T(8,128)(2,1)S(1)} %pad_maximum_fusion.2), channel_id=1, source_target_pairs={{0,0},{1,1},{2,32},{3,33},{4,64},{5,65},{6,96},{7,97},{8,128},{9,1... | collective-permute-start | bytes 196616 | tf_op jit(solution)/shard_map/ppermute | solution.py:328
  14.3 1.9 collective-permute-done.1
  16.2 0.9 pad_maximum_fusion
  17.2 1.6 broadcast_in_dim.15
  18.8 18.7 %all-to-all-start.1 = ((bf16[8,1024,128]{2,1,0:T(8,128)(2,1)}), bf16[8,1024,128]{2,1,0:T(8,128)(2,1)S(1)}, u32[]{:S(2)}, u32[]{:S(2)}) async-start(bf16[8,1024,128]{2,1,0:T(8,128)(2,1)} %broadcast_in_dim.15), calls=%async_computation.1 | async-start | bytes 4194304 | tf_op jit(solution)/shard_map/all_to_all | solution.py:48
  37.5 0.0 copy-done.10
  37.5 27.9 %all-gather = bf16[2176,128]{1,0:T(8,128)(2,1)S(1)} all-gather(bf16[272,128]{1,0:T(8,128)(2,1)S(1)} %pad_maximum_fusion.1), channel_id=2, replica_groups={{0,2,4,6,8,10,12,14},{1,3,5,7,9,11,13,15},{16,18,20,22,24,26,28,30},{17..., dimensions={0}, use_global_device_ids=true | all-gather | bytes 626688 | tf_op jit(solution)/shard_map/all_gather | solution.py:335
  65.5 0.8 all-to-all-done.1.own.w_own_in
  66.3 1.8 broadcast_in_dim.14
  68.1 6.1 %all-to-all-start = ((bf16[4,8,272,128]{3,2,1,0:T(8,128)(2,1)}), bf16[4,8,272,128]{3,2,1,0:T(8,128)(2,1)}, u32[]{:S(2)}, u32[]{:S(2)}) async-start(bf16[4,8,272,128]{3,2,1,0:T(8,128)(2,1)} %broadcast_in_dim.14), calls=%async_computation | async-start | bytes 4456448 | tf_op jit(solution)/shard_map/all_to_all | solution.py:48
  74.2 9.7 %collective-permute-start.2 = (bf16[8,1024,128]{2,1,0:T(8,128)(2,1)S(1)}, bf16[8,1024,128]{2,1,0:T(8,128)(2,1)}, u32[]{:S(2)}, u32[]{:S(2)}) collective-permute-start(bf16[8,1024,128]{2,1,0:T(8,128)(2,1)S(1)} %all-to-all-done.1.own.w_own_in), channel_id=1, source_target_pairs={{0,32},{32,0},{64,96},{96,64},{128,160},{160,128},{192,224},{224,1... | collective-permute-start | bytes 6291464 | tf_op jit(solution)/shard_map/ppermute | solution.py:331
  83.9 3.9 %collective-permute-done.2.other.w_other_in = bf16[8,1024,128]{2,1,0:T(8,128)(2,1)} collective-permute-done((bf16[8,1024,128]{2,1,0:T(8,128)(2,1)S(1)}, bf16[8,1024,128]{2,1,0:T(8,128)(2,1)}, u32[]{:S(2)}, u32[]{:S(2)}) %collective-permute-start.2) | collective-permute-done | bytes 2097184 | tf_op jit(solution)/shard_map/ppermute | solution.py:331
  87.8 13.0 %all-to-all-done = bf16[4,8,272,128]{3,2,1,0:T(8,128)(2,1)} async-done(((bf16[4,8,272,128]{3,2,1,0:T(8,128)(2,1)}), bf16[4,8,272,128]{3,2,1,0:T(8,128)(2,1)}, u32[]{:S(2)}, u32[]{:S(2)}) %all-to-all-start) | async-done | bytes 2228256 | tf_op jit(solution)/shard_map/all_to_all | solution.py:48
  100.7 4.0 %project.1 = (bf16[128,512]{1,0:T(8,128)(2,1)S(1)}, bf16[16,128,512]{2,1,0:T(8,128)(2,1)S(1)}, f32[128,1]{1,0:T(8,128)S(1)}) custom-call(s32[1]{0:T(128)} %bitcast.core_ref, bf16[2,2,8,272,128]{4,3,2,1,0:T(8,128)(2,1)} %bitcast.4.wide.wide_in, bf16[8,1024,128]{2,1,0:T(8,128)(2,1)S(1)} %all-to-all-done.1.own.w_own_in, ...), custom_call_target="tpu_custom_call" | custom-call | tf_op jit(solution)/shard_map/project/pallas_call | solution.py:91
  104.7 0.0 copy-start.2
  104.7 0.6 copy-done.2
  105.4 0.1 broadcast_in_dim.16
  105.4 16.0 %all_to_all.35.own = bf16[8,128,512]{2,1,0:T(8,128)(2,1)S(1)} all-to-all(bf16[8,128,512]{2,1,0:T(8,128)(2,1)S(1)} %broadcast_in_dim.16), channel_id=1, replica_groups={{0,64,128,192,256,320,384,448},{32,96,160,224,288,352,416,480},{1,65,12..., dimensions={0} | all-to-all | bytes 2097152 | tf_op jit(solution)/shard_map/all_to_all | solution.py:48
  121.5 0.0 copy-done.1
  121.5 8.7 %all-to-all-start.3 = ((bf16[16,128,512]{2,1,0:T(8,128)(2,1)}), bf16[16,128,512]{2,1,0:T(8,128)(2,1)S(1)}, u32[]{:S(2)}, u32[]{:S(2)}) async-start(bf16[16,128,512]{2,1,0:T(8,128)(2,1)} %copy-done.1), calls=%async_computation.3 | async-start | bytes 4194304 | tf_op jit(solution)/shard_map/all_to_all | solution.py:341
  130.2 2.3 collective-permute-start.3
  132.5 0.6 convert_element_type.9
  133.1 0.6 pad_add_fusion.place
  133.7 1.0 collective-permute-done.3.other
  134.7 1.0 copy-done.6
  135.7 19.3 %attention.1 = (bf16[2048,384]{1,0:T(8,128)(2,1)}, bf16[2048,128]{1,0:T(8,128)(2,1)}, bf16[4,8,272,128]{3,2,1,0:T(8,128)(2,1)}) custom-call(s32[2]{0:T(128)} %pad_add_fusion.place, f32[1,2048]{1,0:T(1,128)} %bitcast.16, bf16[8,128,512]{2,1,0:T(8,128)(2,1)} %copy-done.3, bf16[8,128,512]{2,1,0:T(8,128)(2,1)} %copy-done.6, ...), custom_call_target="tpu_custom_call" | custom-call | tf_op jit(solution)/shard_map/attention/pallas_call | solution.py:288
  155.0 3.7 %all-to-all-done.3 = bf16[16,128,512]{2,1,0:T(8,128)(2,1)S(1)} async-done(((bf16[16,128,512]{2,1,0:T(8,128)(2,1)}), bf16[16,128,512]{2,1,0:T(8,128)(2,1)S(1)}, u32[]{:S(2)}, u32[]{:S(2)}) %all-to-all-start.3) | async-done | bytes 2097184 | tf_op jit(solution)/shard_map/all_to_all | solution.py:341
  158.7 29.2 %all_to_all.36.parts = bf16[4,8,272,128]{3,2,1,0:T(8,128)(2,1)S(1)} all-to-all(bf16[4,8,272,128]{3,2,1,0:T(8,128)(2,1)} %get-tuple-element.28), channel_id=1, replica_groups={{0,1,16,17},{2,3,18,19},{4,5,20,21},{6,7,22,23},{8,9,24,25},{10,11,26,2..., dimensions={0} | all-to-all | bytes 4456448 | tf_op jit(solution)/shard_map/all_to_all | solution.py:348
  187.9 1.1 merge.1
  189.0 7.4 %all-to-all-start.5 = ((bf16[8,272,128]{2,1,0:T(8,128)(2,1)}), bf16[8,272,128]{2,1,0:T(8,128)(2,1)S(1)}, u32[]{:S(2)}, u32[]{:S(2)}) async-start(bf16[8,272,128]{2,1,0:T(8,128)(2,1)} %merge.1), calls=%async_computation.5 | async-start | bytes 1114112 | tf_op jit(solution)/shard_map/all_to_all | solution.py:349
  196.4 0.5 convolution_convert_fusion
  196.9 0.9 copy-done.5
  197.8 0.7 fusion.1
  198.5 22.2 %all-to-all-done.5.parts = bf16[8,272,128]{2,1,0:T(8,128)(2,1)S(1)} async-done(((bf16[8,272,128]{2,1,0:T(8,128)(2,1)}), bf16[8,272,128]{2,1,0:T(8,128)(2,1)S(1)}, u32[]{:S(2)}, u32[]{:S(2)}) %all-to-all-start.5) | async-done | bytes 557088 | tf_op jit(solution)/shard_map/all_to_all | solution.py:349
  220.7 13.5 %collective-permute-start.4 = (bf16[256,128]{1,0:T(8,128)(2,1)S(1)}, bf16[256,128]{1,0:T(8,128)(2,1)S(1)}, u32[]{:S(2)}, u32[]{:S(2)}) collective-permute-start(bf16[256,128]{1,0:T(8,128)(2,1)S(1)} %convolution_convert_fusion), channel_id=1, source_target_pairs={{0,0},{1,1},{2,32},{3,33},{4,64},{5,65},{6,96},{7,97},{8,128},{9,1... | collective-permute-start | bytes 196616 | tf_op jit(solution)/shard_map/ppermute | solution.py:359
  234.1 1.9 finish.1
  236.0 5.5 %all-to-all-start.6 = ((f32[16,1,128]{2,1,0:T(1,128)}), f32[16,1,128]{2,1,0:T(1,128)S(1)}, u32[]{:S(2)}, u32[]{:S(2)}) async-start(f32[16,1,128]{2,1,0:T(1,128)} %get-tuple-element.36), calls=%async_computation.6 | async-start | bytes 16384 | tf_op jit(solution)/shard_map/all_to_all | solution.py:356
  241.5 0.0 collective-permute-done.4
  241.5 1.9 collective-permute-start.5
  243.5 0.8 fusion.3
  244.2 4.3 %all-to-all-done.6 = f32[16,1,128]{2,1,0:T(1,128)S(1)} async-done(((f32[16,1,128]{2,1,0:T(1,128)}), f32[16,1,128]{2,1,0:T(1,128)S(1)}, u32[]{:S(2)}, u32[]{:S(2)}) %all-to-all-start.6) | async-done | bytes 8224 | tf_op jit(solution)/shard_map/all_to_all | solution.py:356
  248.5 0.5 reduce_sum.9
  249.0 0.0 collective-permute-done.5
  249.1 0.8 copy.15
  (24 shorter events, 0.1 us)
Async XLA Ops:
  1.4 5.7 %collective-permute-start = (bf16[128,128]{1,0:T(8,128)(2,1)S(1)}, bf16[128,128]{1,0:T(8,128)(2,1)S(1)}, u32[]{:S(2)}, u32[]{:S(2)}) collective-permute-start(bf16[128,128]{1,0:T(8,128)(2,1)S(1)} %constant_dynamic-slice_fusion.1), channel_id=1, source_target_pairs={{0,1},{1,0},{2,3},{3,2},{4,5},{5,4},{6,7},{7,6},{8,9},{9,8},{10,11... | collective-permute-start | bytes 98312 | tf_op jit(solution)/shard_map/ppermute | solution.py:326
  7.9 8.4 %collective-permute-start.1 = (bf16[256,128]{1,0:T(8,128)(2,1)S(1)}, bf16[256,128]{1,0:T(8,128)(2,1)S(1)}, u32[]{:S(2)}, u32[]{:S(2)}) collective-permute-start(bf16[256,128]{1,0:T(8,128)(2,1)S(1)} %pad_maximum_fusion.2), channel_id=1, source_target_pairs={{0,0},{1,1},{2,32},{3,33},{4,64},{5,65},{6,96},{7,97},{8,128},{9,1... | collective-permute-start | bytes 196616 | tf_op jit(solution)/shard_map/ppermute | solution.py:328
  18.8 18.7 %copy-start.10 = (bf16[128]{0:T(256)(128)(2,1)S(1)}, bf16[128]{0:T(256)(128)(2,1)}, u32[]{:S(2)}) copy-start(bf16[128]{0:T(256)(128)(2,1)} %param.9) | copy-start | bytes 772
  18.8 18.7 %copy-start.7 = (bf16[128,128]{1,0:T(8,128)(2,1)S(1)}, bf16[128,128]{1,0:T(8,128)(2,1)}, u32[]{:S(2)}) copy-start(bf16[128,128]{1,0:T(8,128)(2,1)} %grad_out.1) | copy-start | bytes 98308
  18.8 18.7 %copy-start.8 = (bf16[128,128]{1,0:T(8,128)(2,1)S(1)}, bf16[128,128]{1,0:T(8,128)(2,1)}, u32[]{:S(2)}) copy-start(bf16[128,128]{1,0:T(8,128)(2,1)} %hidden.1) | copy-start | bytes 98308
  18.8 47.5 %all-to-all-start.1 = ((bf16[8,1024,128]{2,1,0:T(8,128)(2,1)}), bf16[8,1024,128]{2,1,0:T(8,128)(2,1)S(1)}, u32[]{:S(2)}, u32[]{:S(2)}) async-start(bf16[8,1024,128]{2,1,0:T(8,128)(2,1)} %broadcast_in_dim.15), calls=%async_computation.1 | async-start | bytes 4194304 | tf_op jit(solution)/shard_map/all_to_all | solution.py:48
  66.3 34.5 %copy-start = (bf16[8,1024,128]{2,1,0:T(8,128)(2,1)}, bf16[8,1024,128]{2,1,0:T(8,128)(2,1)S(1)}, u32[]{:S(2)}) copy-start(bf16[8,1024,128]{2,1,0:T(8,128)(2,1)S(1)} %all-to-all-done.1.own.w_own_in) | copy-start | bytes 6291460
  68.1 32.6 %all-to-all-start = ((bf16[4,8,272,128]{3,2,1,0:T(8,128)(2,1)}), bf16[4,8,272,128]{3,2,1,0:T(8,128)(2,1)}, u32[]{:S(2)}, u32[]{:S(2)}) async-start(bf16[4,8,272,128]{3,2,1,0:T(8,128)(2,1)} %broadcast_in_dim.14), calls=%async_computation | async-start | bytes 4456448 | tf_op jit(solution)/shard_map/all_to_all | solution.py:48
  74.2 13.6 %collective-permute-start.2 = (bf16[8,1024,128]{2,1,0:T(8,128)(2,1)S(1)}, bf16[8,1024,128]{2,1,0:T(8,128)(2,1)}, u32[]{:S(2)}, u32[]{:S(2)}) collective-permute-start(bf16[8,1024,128]{2,1,0:T(8,128)(2,1)S(1)} %all-to-all-done.1.own.w_own_in), channel_id=1, source_target_pairs={{0,32},{32,0},{64,96},{96,64},{128,160},{160,128},{192,224},{224,1... | collective-permute-start | bytes 6291464 | tf_op jit(solution)/shard_map/ppermute | solution.py:331
  104.7 0.6 copy-start.2
  105.4 16.1 %copy-start.1 = (bf16[16,128,512]{2,1,0:T(8,128)(2,1)}, bf16[16,128,512]{2,1,0:T(8,128)(2,1)S(1)}, u32[]{:S(2)}) copy-start(bf16[16,128,512]{2,1,0:T(8,128)(2,1)S(1)} %get-tuple-element.27) | copy-start | bytes 6291460
  121.5 8.7 %copy-start.3 = (bf16[8,128,512]{2,1,0:T(8,128)(2,1)}, bf16[8,128,512]{2,1,0:T(8,128)(2,1)S(1)}, u32[]{:S(2)}) copy-start(bf16[8,128,512]{2,1,0:T(8,128)(2,1)S(1)} %all_to_all.35.own) | copy-start | bytes 3145732
  121.5 11.0 %copy-start.9 = (s32[2048]{0:T(1024)S(1)}, s32[2048]{0:T(1024)}, u32[]{:S(2)}) copy-start(s32[2048]{0:T(1024)} %param.14) | copy-start | bytes 24580
  121.5 37.2 %all-to-all-start.3 = ((bf16[16,128,512]{2,1,0:T(8,128)(2,1)}), bf16[16,128,512]{2,1,0:T(8,128)(2,1)S(1)}, u32[]{:S(2)}, u32[]{:S(2)}) async-start(bf16[16,128,512]{2,1,0:T(8,128)(2,1)} %copy-done.1), calls=%async_computation.3 | async-start | bytes 4194304 | tf_op jit(solution)/shard_map/all_to_all | solution.py:341
  130.2 4.6 %collective-permute-start.3 = (bf16[8,128,512]{2,1,0:T(8,128)(2,1)S(1)}, bf16[8,128,512]{2,1,0:T(8,128)(2,1)S(1)}, u32[]{:S(2)}, u32[]{:S(2)}) collective-permute-start(bf16[8,128,512]{2,1,0:T(8,128)(2,1)S(1)} %all_to_all.35.own), channel_id=1, source_target_pairs={{0,32},{32,0},{64,96},{96,64},{128,160},{160,128},{192,224},{224,1... | collective-permute-start | bytes 3145736 | tf_op jit(solution)/shard_map/ppermute | solution.py:343
  134.7 1.0 copy-start.6
  187.9 8.5 %copy-start.11 = (bf16[2048,128]{1,0:T(8,128)(2,1)S(1)}, bf16[2048,128]{1,0:T(8,128)(2,1)}, u32[]{:S(2)}) copy-start(bf16[2048,128]{1,0:T(8,128)(2,1)} %get-tuple-element.31) | copy-start | bytes 1572868
  189.0 31.7 %all-to-all-start.5 = ((bf16[8,272,128]{2,1,0:T(8,128)(2,1)}), bf16[8,272,128]{2,1,0:T(8,128)(2,1)S(1)}, u32[]{:S(2)}, u32[]{:S(2)}) async-start(bf16[8,272,128]{2,1,0:T(8,128)(2,1)} %merge.1), calls=%async_computation.5 | async-start | bytes 1114112 | tf_op jit(solution)/shard_map/all_to_all | solution.py:349
  196.4 1.4 copy-start.5
  220.7 13.5 %copy-start.4 = (bf16[8,272,128]{2,1,0:T(8,128)(2,1)}, bf16[8,272,128]{2,1,0:T(8,128)(2,1)S(1)}, u32[]{:S(2)}) copy-start(bf16[8,272,128]{2,1,0:T(8,128)(2,1)S(1)} %all-to-all-done.5.parts) | copy-start | bytes 1671172
  220.7 20.8 %collective-permute-start.4 = (bf16[256,128]{1,0:T(8,128)(2,1)S(1)}, bf16[256,128]{1,0:T(8,128)(2,1)S(1)}, u32[]{:S(2)}, u32[]{:S(2)}) collective-permute-start(bf16[256,128]{1,0:T(8,128)(2,1)S(1)} %convolution_convert_fusion), channel_id=1, source_target_pairs={{0,0},{1,1},{2,32},{3,33},{4,64},{5,65},{6,96},{7,97},{8,128},{9,1... | collective-permute-start | bytes 196616 | tf_op jit(solution)/shard_map/ppermute | solution.py:359
  236.0 12.5 %all-to-all-start.6 = ((f32[16,1,128]{2,1,0:T(1,128)}), f32[16,1,128]{2,1,0:T(1,128)S(1)}, u32[]{:S(2)}, u32[]{:S(2)}) async-start(f32[16,1,128]{2,1,0:T(1,128)} %get-tuple-element.36), calls=%async_computation.6 | async-start | bytes 16384 | tf_op jit(solution)/shard_map/all_to_all | solution.py:356
  241.5 7.5 %collective-permute-start.5 = (bf16[128,128]{1,0:T(8,128)(2,1)S(1)}, bf16[128,128]{1,0:T(8,128)(2,1)S(1)}, u32[]{:S(2)}, u32[]{:S(2)}) collective-permute-start(bf16[128,128]{1,0:T(8,128)(2,1)S(1)} %constant_dynamic-slice_fusion), channel_id=1, source_target_pairs={{0,1},{1,0},{2,3},{3,2},{4,5},{5,4},{6,7},{7,6},{8,9},{9,8},{10,11... | collective-permute-start | bytes 98312 | tf_op jit(solution)/shard_map/ppermute | solution.py:362

commit v3 on v2

--- a/solution.py
+++ b/solution.py
@@ -8,7 +8,7 @@
 D = 4096
 HD = 128
 TOK = 2048
-BLOCK = 256
+BLOCK = 512
 OVER = 128
 SCALE = HD ** (-0.5)
 MASKED = -1e30
@@ -52,7 +52,15 @@
     return x.astype(F32).T.astype(BF16)
 
 
-def project_kernel(core_ref, wide, own, other, heads, both, recip_out):
+def project_kernel(
+    core_ref, wide, own_in, other_in, heads, both, recip_out, own, other, sems
+):
+    copies = [
+        pltpu.make_async_copy(own_in, own, sems.at[0]),
+        pltpu.make_async_copy(other_in, other, sems.at[1]),
+    ]
+    for copy in copies:
+        copy.start()
     core = core_ref[0]
     squares = jnp.zeros((128, 128), F32)
     for a in range(2):
@@ -62,6 +70,8 @@
                 squares = squares + x * x
     recip = lax.rsqrt(jnp.sum(squares, axis=1, keepdims=True) / D + norm_eps)
     recip_out[...] = recip
+    for copy in copies:
+        copy.wait()
     qkv = jnp.zeros((128, 3 * HD), F32)
     grad = jnp.zeros((128, HD), F32)
     for k in range(8):
@@ -95,8 +105,14 @@
             jax.ShapeDtypeStruct((16, 128, 512), BF16),
             jax.ShapeDtypeStruct((128, 1), F32),
         ),
-        in_specs=[pl.BlockSpec(memory_space=pltpu.SMEM), vmem, vmem, vmem],
+        in_specs=[pl.BlockSpec(memory_space=pltpu.SMEM), vmem]
+        + [pl.BlockSpec(memory_space=pl.ANY)] * 2,
         out_specs=(vmem, vmem, vmem),
+        scratch_shapes=[
+            pltpu.VMEM(own.shape, BF16),
+            pltpu.VMEM(other.shape, BF16),
+            pltpu.SemaphoreType.DMA((2,)),
+        ],
         compiler_params=pltpu.CompilerParams(vmem_limit_bytes=48 * 1024 * 1024),
         name="project",
     )(core[None], wide, own, other)
@@ -165,7 +181,7 @@
 
 def attention_kernel(
     place, ids, own, other, wide_in, w_own_in, w_other_in, grads, att, parts,
-    q_s, k_s, v_s, g_s, q_t, k_t, v_t, g_t, s_s, e_s, dk_s, dv_s,
+    q_s, k_s, v_s, k_t, v_t, g_t, s_s, e_s, dk_s, dv_s,
     wide, w_own, w_other, sems,
 ):
     core, row = place[0], place[1]
@@ -180,10 +196,13 @@
     for k in range(8):
         for src, flag in ((own, core), (other, 1 - core)):
             at = pl.ds(pl.multiple_of((2 * k + flag) * 128, 128), 128)
-            for n, (flat, turned) in enumerate(((q_s, q_t), (k_s, k_t), (v_s, v_t), (g_s, g_t))):
-                piece = src[k, :, n * 128 : (n + 1) * 128]
-                flat[at, :] = piece
-                turned[:, at] = flip(piece)
+            query, key, value, grad = [src[k, :, n * 128 : (n + 1) * 128] for n in range(4)]
+            q_s[at, :] = query
+            k_s[at, :] = key
+            v_s[at, :] = value
+            k_t[:, at] = flip(key)
+            v_t[:, at] = flip(value)
+            g_t[:, at] = flip(grad)
     dk_s[...] = jnp.zeros_like(dk_s)
     dv_s[...] = jnp.zeros_like(dv_s)
 
@@ -198,7 +217,7 @@
         here = slice(base, base + BLOCK)
         top = jnp.full((1, BLOCK), MASKED, F32)
         for start, size in tiles_of(i):
-            score = mm(k_s[start : start + size, :], q_t[:, here])
+            score = mm_nt(k_s[start : start + size, :], q_s[here, :])
             if start >= base:
                 ids_tile = jnp.broadcast_to(ids[:, start : start + size], (8, size))
                 seen = ids_tile.T[:, 0:1] <= ids[:, here]
@@ -217,7 +236,6 @@
         for start, size in tiles_of(i):
             at = slice(start, start + size)
             part = jnp.exp((s_s[i % 2, at, :] - top) * SCALE)
-            s_s[i % 2, at, :] = part
             total = total + jnp.sum(part, axis=0, keepdims=True)
             low = part.astype(BF16)
             e_s[i % 2, at, :] = low
@@ -235,7 +253,7 @@
         for start, size in tiles_of(i):
             at = slice(start, start + size)
             dprob = mm(v_s[at, :], grad_t)
-            dscore = (s_s[i % 2, at, :] * (dprob - delta)).astype(BF16)
+            dscore = (e_s[i % 2, at, :].astype(F32) * (dprob - delta)).astype(BF16)
             dq_t = dq_t + mm(k_t[:, at], dscore)
             dk_s[at, :] += mm(dscore, query)
             dv_s[at, :] += mm(e_s[i % 2, at, :], grad)
@@ -294,8 +312,8 @@
         ),
         in_specs=[pl.BlockSpec(memory_space=pltpu.SMEM)] + [vmem] * 3 + [anywhere] * 3,
         out_specs=(vmem, vmem, vmem),
-        scratch_shapes=[low] * 4
-        + [low_t] * 4
+        scratch_shapes=[low] * 3
+        + [low_t] * 3
         + [
             pltpu.VMEM((2, TOK, BLOCK), F32),
             pltpu.VMEM((2, TOK, BLOCK), BF16),
@@ -353,6 +371,7 @@
     parts, grad_w, grad_o = lax.optimization_barrier((parts, grad_w, grad_o))
 
     mixed, grad_x, gain_part = finish(parts, hidden_in, norm_gain, recip, grad_out)
+    gain_part, grad_o = lax.optimization_barrier((gain_part, grad_o))
     gain_all = lax.all_to_all(gain_part, "row", 0, 0, tiled=True)
     grad_gain = jnp.sum(gain_all, axis=(0, 1))
 

time: 252 us -> 255 us (1.012)
  transfers between devices with their start and end apart: 11 -> 11, of which waited for: 9 -> 9; matrix products, arithmetic and copies ran while one was open for 1% -> 1% of each run, Pallas kernels for 8% -> 7%
where the time goes in v3:
time: 255 us; the launch traced here: 252 us
  starting transfers between devices  84.5 us (33%)
  blocking collectives  73.1 us (29%)
  waiting for transfers between devices  54.4 us (21%)
  Pallas kernels  24.7 us (10%)
  local copies, waits for them, and re-layouts  9.17 us (4%)
  other arithmetic  3.47 us (1%)
    all_to_all x1, blocking collectives, local(): lax.all_to_all(parts, 'col', 0, 0, tiled=True, axis_index_groups=NEAR)  29.2 us
    all_gather x1, blocking collectives, local(): far = lax.all_gather(pair, 'col', axis=0, axis_index_groups=FAR)  27.9 us
    all_to_all x2, starting transfers between devices, spread(): lax.all_to_all(wide, axis, 0, 0, tiled=True, axis_index_groups=groups)  24.8 us
    all_to_all x1, waiting for transfers between devices, local(): lax.all_to_all(merge(parts), 'col', 0, 0, tiled=True, axis_index_groups=FAR)  22.2 us
    pallas_call x1, Pallas kernels, attention(): pl.pallas_call(attention_kernel, out_shape=(jax.ShapeDtypeStruct((TOK, 3...  16.9 us
    all_to_all x1, blocking collectives, spread(): lax.all_to_all(wide, axis, 0, 0, tiled=True, axis_index_groups=groups)  16 us
    all_to_all x2, waiting for transfers between devices, spread(): lax.all_to_all(wide, axis, 0, 0, tiled=True, axis_index_groups=groups)  13.8 us
    ppermute x1, starting transfers between devices, local(): grad_o = lax.ppermute(grad_o, ('row', 'col'), TURN)  13.5 us
  transfers between devices with their start and end apart: 11, of which 9 were waited for; matrix products, arithmetic and copies ran while one was open for 1% of the time, Pallas kernels for 7%

profile of v3, /device:TPU:1, one launch (start us, length us, event | category | flops | bytes accessed | tf_op | source)
XLA Modules:
  0.0 251.5 jit_solution(17806232360451995025)
XLA Ops:
  0.6 0.8 constant_dynamic-slice_fusion.1
  1.4 4.4 %collective-permute-start = (bf16[128,128]{1,0:T(8,128)(2,1)S(1)}, bf16[128,128]{1,0:T(8,128)(2,1)S(1)}, u32[]{:S(2)}, u32[]{:S(2)}) collective-permute-start(bf16[128,128]{1,0:T(8,128)(2,1)S(1)} %constant_dynamic-slice_fusion.1), channel_id=1, source_target_pairs={{0,1},{1,0},{2,3},{3,2},{4,5},{5,4},{6,7},{7,6},{8,9},{9,8},{10,11... | collective-permute-start | bytes 98312 | tf_op jit(solution)/shard_map/ppermute | solution.py:344
  5.8 1.3 collective-permute-done
  7.1 0.8 broadcast_select_fusion.1
  7.9 6.4 %collective-permute-start.1 = (bf16[256,128]{1,0:T(8,128)(2,1)S(1)}, bf16[256,128]{1,0:T(8,128)(2,1)S(1)}, u32[]{:S(2)}, u32[]{:S(2)}) collective-permute-start(bf16[256,128]{1,0:T(8,128)(2,1)S(1)} %pad_maximum_fusion.2), channel_id=1, source_target_pairs={{0,0},{1,1},{2,32},{3,33},{4,64},{5,65},{6,96},{7,97},{8,128},{9,1... | collective-permute-start | bytes 196616 | tf_op jit(solution)/shard_map/ppermute | solution.py:346
  14.3 1.9 collective-permute-done.1
  16.2 0.9 pad_maximum_fusion
  17.2 1.6 broadcast_in_dim.15
  18.8 18.7 %all-to-all-start.1 = ((bf16[8,1024,128]{2,1,0:T(8,128)(2,1)}), bf16[8,1024,128]{2,1,0:T(8,128)(2,1)S(1)}, u32[]{:S(2)}, u32[]{:S(2)}) async-start(bf16[8,1024,128]{2,1,0:T(8,128)(2,1)} %broadcast_in_dim.15), calls=%async_computation.1 | async-start | bytes 4194304 | tf_op jit(solution)/shard_map/all_to_all | solution.py:48
  37.5 0.0 copy-done.7
  37.5 27.9 %all-gather = bf16[2176,128]{1,0:T(8,128)(2,1)S(1)} all-gather(bf16[272,128]{1,0:T(8,128)(2,1)S(1)} %pad_maximum_fusion.1), channel_id=2, replica_groups={{0,2,4,6,8,10,12,14},{1,3,5,7,9,11,13,15},{16,18,20,22,24,26,28,30},{17..., dimensions={0}, use_global_device_ids=true | all-gather | bytes 626688 | tf_op jit(solution)/shard_map/all_gather | solution.py:353
  65.5 0.8 all-to-all-done.1.own_in.w_own_in
  66.3 1.8 broadcast_in_dim.14
  68.1 6.1 %all-to-all-start = ((bf16[4,8,272,128]{3,2,1,0:T(8,128)(2,1)}), bf16[4,8,272,128]{3,2,1,0:T(8,128)(2,1)}, u32[]{:S(2)}, u32[]{:S(2)}) async-start(bf16[4,8,272,128]{3,2,1,0:T(8,128)(2,1)} %broadcast_in_dim.14), calls=%async_computation | async-start | bytes 4456448 | tf_op jit(solution)/shard_map/all_to_all | solution.py:48
  74.2 9.7 %collective-permute-start.2 = (bf16[8,1024,128]{2,1,0:T(8,128)(2,1)S(1)}, bf16[8,1024,128]{2,1,0:T(8,128)(2,1)}, u32[]{:S(2)}, u32[]{:S(2)}) collective-permute-start(bf16[8,1024,128]{2,1,0:T(8,128)(2,1)S(1)} %all-to-all-done.1.own_in.w_own_in), channel_id=1, source_target_pairs={{0,32},{32,0},{64,96},{96,64},{128,160},{160,128},{192,224},{224,1... | collective-permute-start | bytes 6291464 | tf_op jit(solution)/shard_map/ppermute | solution.py:349
  83.9 3.9 %collective-permute-done.2.other_in.w_other_in = bf16[8,1024,128]{2,1,0:T(8,128)(2,1)} collective-permute-done((bf16[8,1024,128]{2,1,0:T(8,128)(2,1)S(1)}, bf16[8,1024,128]{2,1,0:T(8,128)(2,1)}, u32[]{:S(2)}, u32[]{:S(2)}) %collective-permute-start.2) | collective-permute-done | bytes 2097184 | tf_op jit(solution)/shard_map/ppermute | solution.py:349
  87.8 13.0 %all-to-all-done = bf16[4,8,272,128]{3,2,1,0:T(8,128)(2,1)} async-done(((bf16[4,8,272,128]{3,2,1,0:T(8,128)(2,1)}), bf16[4,8,272,128]{3,2,1,0:T(8,128)(2,1)}, u32[]{:S(2)}, u32[]{:S(2)}) %all-to-all-start) | async-done | bytes 2228256 | tf_op jit(solution)/shard_map/all_to_all | solution.py:48
  100.7 4.9 %project.1 = (bf16[128,512]{1,0:T(8,128)(2,1)S(1)}, bf16[16,128,512]{2,1,0:T(8,128)(2,1)S(1)}, f32[128,1]{1,0:T(8,128)S(1)}) custom-call(s32[1]{0:T(128)} %bitcast.core_ref, bf16[2,2,8,272,128]{4,3,2,1,0:T(8,128)(2,1)} %bitcast.4.wide.wide_in, bf16[8,1024,128]{2,1,0:T(8,128)(2,1)S(1)} %all-to-all-done.1.own_in.w_own_in, ...), custom_call_target="tpu_custom_call" | custom-call | tf_op jit(solution)/shard_map/project/pallas_call | solution.py:101
  105.6 0.0 copy-start.2
  105.6 0.6 copy-done.2
  106.2 0.1 broadcast_in_dim.16
  106.3 16.0 %all_to_all.35.own = bf16[8,128,512]{2,1,0:T(8,128)(2,1)S(1)} all-to-all(bf16[8,128,512]{2,1,0:T(8,128)(2,1)S(1)} %broadcast_in_dim.16), channel_id=1, replica_groups={{0,64,128,192,256,320,384,448},{32,96,160,224,288,352,416,480},{1,65,12..., dimensions={0} | all-to-all | bytes 2097152 | tf_op jit(solution)/shard_map/all_to_all | solution.py:48
  122.3 8.7 %all-to-all-start.3 = ((bf16[16,128,512]{2,1,0:T(8,128)(2,1)}), bf16[16,128,512]{2,1,0:T(8,128)(2,1)S(1)}, u32[]{:S(2)}, u32[]{:S(2)}) async-start(bf16[16,128,512]{2,1,0:T(8,128)(2,1)} %copy-done.1), calls=%async_computation.3 | async-start | bytes 4194304 | tf_op jit(solution)/shard_map/all_to_all | solution.py:359
  131.1 2.3 collective-permute-start.3
  133.4 0.6 convert_element_type.9
  134.0 0.6 pad_add_fusion.place
  134.6 1.0 collective-permute-done.3.other
  135.6 1.0 copy-done.6
  136.6 16.9 %attention.1 = (bf16[2048,384]{1,0:T(8,128)(2,1)}, bf16[2048,128]{1,0:T(8,128)(2,1)}, bf16[4,8,272,128]{3,2,1,0:T(8,128)(2,1)}) custom-call(s32[2]{0:T(128)} %pad_add_fusion.place, f32[1,2048]{1,0:T(1,128)} %bitcast.16, bf16[8,128,512]{2,1,0:T(8,128)(2,1)} %copy-done.3, bf16[8,128,512]{2,1,0:T(8,128)(2,1)} %copy-done.6, ...), custom_call_target="tpu_custom_call" | custom-call | tf_op jit(solution)/shard_map/attention/pallas_call | solution.py:306
  153.5 6.1 %all-to-all-done.3 = bf16[16,128,512]{2,1,0:T(8,128)(2,1)S(1)} async-done(((bf16[16,128,512]{2,1,0:T(8,128)(2,1)}), bf16[16,128,512]{2,1,0:T(8,128)(2,1)S(1)}, u32[]{:S(2)}, u32[]{:S(2)}) %all-to-all-start.3) | async-done | bytes 2097184 | tf_op jit(solution)/shard_map/all_to_all | solution.py:359
  159.6 29.2 %all_to_all.36.parts = bf16[4,8,272,128]{3,2,1,0:T(8,128)(2,1)S(1)} all-to-all(bf16[4,8,272,128]{3,2,1,0:T(8,128)(2,1)} %get-tuple-element.30), channel_id=1, replica_groups={{0,1,16,17},{2,3,18,19},{4,5,20,21},{6,7,22,23},{8,9,24,25},{10,11,26,2..., dimensions={0} | all-to-all | bytes 4456448 | tf_op jit(solution)/shard_map/all_to_all | solution.py:366
  188.8 1.1 merge.1
  189.9 7.4 %all-to-all-start.5 = ((bf16[8,272,128]{2,1,0:T(8,128)(2,1)}), bf16[8,272,128]{2,1,0:T(8,128)(2,1)S(1)}, u32[]{:S(2)}, u32[]{:S(2)}) async-start(bf16[8,272,128]{2,1,0:T(8,128)(2,1)} %merge.1), calls=%async_computation.5 | async-start | bytes 1114112 | tf_op jit(solution)/shard_map/all_to_all | solution.py:367
  197.3 0.5 convolution_convert_fusion
  197.8 0.9 copy-done.5
  198.7 0.7 fusion.1
  199.4 22.2 %all-to-all-done.5.parts = bf16[8,272,128]{2,1,0:T(8,128)(2,1)S(1)} async-done(((bf16[8,272,128]{2,1,0:T(8,128)(2,1)}), bf16[8,272,128]{2,1,0:T(8,128)(2,1)S(1)}, u32[]{:S(2)}, u32[]{:S(2)}) %all-to-all-start.5) | async-done | bytes 557088 | tf_op jit(solution)/shard_map/all_to_all | solution.py:367
  221.6 0.8 copy-done.4
  222.4 1.9 finish.1
  224.3 13.5 %collective-permute-start.4 = (bf16[256,128]{1,0:T(8,128)(2,1)S(1)}, bf16[256,128]{1,0:T(8,128)(2,1)S(1)}, u32[]{:S(2)}, u32[]{:S(2)}) collective-permute-start(bf16[256,128]{1,0:T(8,128)(2,1)S(1)} %convolution_convert_fusion), channel_id=1, source_target_pairs={{0,0},{1,1},{2,32},{3,33},{4,64},{5,65},{6,96},{7,97},{8,128},{9,1... | collective-permute-start | bytes 196616 | tf_op jit(solution)/shard_map/ppermute | solution.py:378
  237.7 5.5 %all-to-all-start.6 = ((f32[16,1,128]{2,1,0:T(1,128)}), f32[16,1,128]{2,1,0:T(1,128)S(1)}, u32[]{:S(2)}, u32[]{:S(2)}) async-start(f32[16,1,128]{2,1,0:T(1,128)} %get-tuple-element.40), calls=%async_computation.6 | async-start | bytes 16384 | tf_op jit(solution)/shard_map/all_to_all | solution.py:375
  243.2 0.0 collective-permute-done.4
  243.2 1.9 collective-permute-start.5
  245.2 0.8 fusion.3
  245.9 4.3 %all-to-all-done.6 = f32[16,1,128]{2,1,0:T(1,128)S(1)} async-done(((f32[16,1,128]{2,1,0:T(1,128)}), f32[16,1,128]{2,1,0:T(1,128)S(1)}, u32[]{:S(2)}, u32[]{:S(2)}) %all-to-all-start.6) | async-done | bytes 8224 | tf_op jit(solution)/shard_map/all_to_all | solution.py:375
  250.2 0.5 reduce_sum.9
  250.7 0.0 collective-permute-done.5
  250.8 0.8 copy.15
  (24 shorter events, 0.1 us)
Async XLA Ops:
  1.4 5.7 %collective-permute-start = (bf16[128,128]{1,0:T(8,128)(2,1)S(1)}, bf16[128,128]{1,0:T(8,128)(2,1)S(1)}, u32[]{:S(2)}, u32[]{:S(2)}) collective-permute-start(bf16[128,128]{1,0:T(8,128)(2,1)S(1)} %constant_dynamic-slice_fusion.1), channel_id=1, source_target_pairs={{0,1},{1,0},{2,3},{3,2},{4,5},{5,4},{6,7},{7,6},{8,9},{9,8},{10,11... | collective-permute-start | bytes 98312 | tf_op jit(solution)/shard_map/ppermute | solution.py:344
  7.9 8.4 %collective-permute-start.1 = (bf16[256,128]{1,0:T(8,128)(2,1)S(1)}, bf16[256,128]{1,0:T(8,128)(2,1)S(1)}, u32[]{:S(2)}, u32[]{:S(2)}) collective-permute-start(bf16[256,128]{1,0:T(8,128)(2,1)S(1)} %pad_maximum_fusion.2), channel_id=1, source_target_pairs={{0,0},{1,1},{2,32},{3,33},{4,64},{5,65},{6,96},{7,97},{8,128},{9,1... | collective-permute-start | bytes 196616 | tf_op jit(solution)/shard_map/ppermute | solution.py:346
  18.8 18.7 %copy-start.10 = (bf16[128]{0:T(256)(128)(2,1)S(1)}, bf16[128]{0:T(256)(128)(2,1)}, u32[]{:S(2)}) copy-start(bf16[128]{0:T(256)(128)(2,1)} %param.9) | copy-start | bytes 772
  18.8 18.7 %copy-start.7 = (bf16[128,128]{1,0:T(8,128)(2,1)S(1)}, bf16[128,128]{1,0:T(8,128)(2,1)}, u32[]{:S(2)}) copy-start(bf16[128,128]{1,0:T(8,128)(2,1)} %grad_out.1) | copy-start | bytes 98308
  18.8 18.7 %copy-start.8 = (bf16[128,128]{1,0:T(8,128)(2,1)S(1)}, bf16[128,128]{1,0:T(8,128)(2,1)}, u32[]{:S(2)}) copy-start(bf16[128,128]{1,0:T(8,128)(2,1)} %hidden.1) | copy-start | bytes 98308
  18.8 47.5 %all-to-all-start.1 = ((bf16[8,1024,128]{2,1,0:T(8,128)(2,1)}), bf16[8,1024,128]{2,1,0:T(8,128)(2,1)S(1)}, u32[]{:S(2)}, u32[]{:S(2)}) async-start(bf16[8,1024,128]{2,1,0:T(8,128)(2,1)} %broadcast_in_dim.15), calls=%async_computation.1 | async-start | bytes 4194304 | tf_op jit(solution)/shard_map/all_to_all | solution.py:48
  66.3 34.5 %copy-start = (bf16[8,1024,128]{2,1,0:T(8,128)(2,1)}, bf16[8,1024,128]{2,1,0:T(8,128)(2,1)S(1)}, u32[]{:S(2)}) copy-start(bf16[8,1024,128]{2,1,0:T(8,128)(2,1)S(1)} %all-to-all-done.1.own_in.w_own_in) | copy-start | bytes 6291460
  68.1 32.6 %all-to-all-start = ((bf16[4,8,272,128]{3,2,1,0:T(8,128)(2,1)}), bf16[4,8,272,128]{3,2,1,0:T(8,128)(2,1)}, u32[]{:S(2)}, u32[]{:S(2)}) async-start(bf16[4,8,272,128]{3,2,1,0:T(8,128)(2,1)} %broadcast_in_dim.14), calls=%async_computation | async-start | bytes 4456448 | tf_op jit(solution)/shard_map/all_to_all | solution.py:48
  74.2 13.6 %collective-permute-start.2 = (bf16[8,1024,128]{2,1,0:T(8,128)(2,1)S(1)}, bf16[8,1024,128]{2,1,0:T(8,128)(2,1)}, u32[]{:S(2)}, u32[]{:S(2)}) collective-permute-start(bf16[8,1024,128]{2,1,0:T(8,128)(2,1)S(1)} %all-to-all-done.1.own_in.w_own_in), channel_id=1, source_target_pairs={{0,32},{32,0},{64,96},{96,64},{128,160},{160,128},{192,224},{224,1... | collective-permute-start | bytes 6291464 | tf_op jit(solution)/shard_map/ppermute | solution.py:349
  105.6 0.6 copy-start.2
  106.2 16.1 %copy-start.1 = (bf16[16,128,512]{2,1,0:T(8,128)(2,1)}, bf16[16,128,512]{2,1,0:T(8,128)(2,1)S(1)}, u32[]{:S(2)}) copy-start(bf16[16,128,512]{2,1,0:T(8,128)(2,1)S(1)} %get-tuple-element.29) | copy-start | bytes 6291460
  122.3 8.7 %copy-start.3 = (bf16[8,128,512]{2,1,0:T(8,128)(2,1)}, bf16[8,128,512]{2,1,0:T(8,128)(2,1)S(1)}, u32[]{:S(2)}) copy-start(bf16[8,128,512]{2,1,0:T(8,128)(2,1)S(1)} %all_to_all.35.own) | copy-start | bytes 3145732
  122.3 11.1 %copy-start.9 = (s32[2048]{0:T(1024)S(1)}, s32[2048]{0:T(1024)}, u32[]{:S(2)}) copy-start(s32[2048]{0:T(1024)} %param.14) | copy-start | bytes 24580
  122.3 37.2 %all-to-all-start.3 = ((bf16[16,128,512]{2,1,0:T(8,128)(2,1)}), bf16[16,128,512]{2,1,0:T(8,128)(2,1)S(1)}, u32[]{:S(2)}, u32[]{:S(2)}) async-start(bf16[16,128,512]{2,1,0:T(8,128)(2,1)} %copy-done.1), calls=%async_computation.3 | async-start | bytes 4194304 | tf_op jit(solution)/shard_map/all_to_all | solution.py:359
  131.1 4.6 %collective-permute-start.3 = (bf16[8,128,512]{2,1,0:T(8,128)(2,1)S(1)}, bf16[8,128,512]{2,1,0:T(8,128)(2,1)S(1)}, u32[]{:S(2)}, u32[]{:S(2)}) collective-permute-start(bf16[8,128,512]{2,1,0:T(8,128)(2,1)S(1)} %all_to_all.35.own), channel_id=1, source_target_pairs={{0,32},{32,0},{64,96},{96,64},{128,160},{160,128},{192,224},{224,1... | collective-permute-start | bytes 3145736 | tf_op jit(solution)/shard_map/ppermute | solution.py:361
  135.6 1.0 copy-start.6
  188.8 8.5 %copy-start.11 = (bf16[2048,128]{1,0:T(8,128)(2,1)S(1)}, bf16[2048,128]{1,0:T(8,128)(2,1)}, u32[]{:S(2)}) copy-start(bf16[2048,128]{1,0:T(8,128)(2,1)} %get-tuple-element.33) | copy-start | bytes 1572868
  189.9 31.7 %all-to-all-start.5 = ((bf16[8,272,128]{2,1,0:T(8,128)(2,1)}), bf16[8,272,128]{2,1,0:T(8,128)(2,1)S(1)}, u32[]{:S(2)}, u32[]{:S(2)}) async-start(bf16[8,272,128]{2,1,0:T(8,128)(2,1)} %merge.1), calls=%async_computation.5 | async-start | bytes 1114112 | tf_op jit(solution)/shard_map/all_to_all | solution.py:367
  197.3 1.4 copy-start.5
  221.6 0.8 copy-start.4
  224.3 18.9 %collective-permute-start.4 = (bf16[256,128]{1,0:T(8,128)(2,1)S(1)}, bf16[256,128]{1,0:T(8,128)(2,1)S(1)}, u32[]{:S(2)}, u32[]{:S(2)}) collective-permute-start(bf16[256,128]{1,0:T(8,128)(2,1)S(1)} %convolution_convert_fusion), channel_id=1, source_target_pairs={{0,0},{1,1},{2,32},{3,33},{4,64},{5,65},{6,96},{7,97},{8,128},{9,1... | collective-permute-start | bytes 196616 | tf_op jit(solution)/shard_map/ppermute | solution.py:378
  237.7 12.5 %all-to-all-start.6 = ((f32[16,1,128]{2,1,0:T(1,128)}), f32[16,1,128]{2,1,0:T(1,128)S(1)}, u32[]{:S(2)}, u32[]{:S(2)}) async-start(f32[16,1,128]{2,1,0:T(1,128)} %get-tuple-element.40), calls=%async_computation.6 | async-start | bytes 16384 | tf_op jit(solution)/shard_map/all_to_all | solution.py:375
  243.2 7.5 %collective-permute-start.5 = (bf16[128,128]{1,0:T(8,128)(2,1)S(1)}, bf16[128,128]{1,0:T(8,128)(2,1)S(1)}, u32[]{:S(2)}, u32[]{:S(2)}) collective-permute-start(bf16[128,128]{1,0:T(8,128)(2,1)S(1)} %constant_dynamic-slice_fusion), channel_id=1, source_target_pairs={{0,1},{1,0},{2,3},{3,2},{4,5},{5,4},{6,7},{7,6},{8,9},{9,8},{10,11... | collective-permute-start | bytes 98312 | tf_op jit(solution)/shard_map/ppermute | solution.py:381
